TPU v7x, 32 devices: a whole 2x2x4 slice. The times are simulated.
32 devices in a mesh: section: 2 (over x), lat: 8 (over z, y), lon: 2 (over core).
Axes of the slice: x: 2, y: 2, z: 4, core: 2. Of those that a mesh axis runs over, the one named last changes fastest.
Arguments:
- block_hidden: bfloat16 [2, 48, 768, 512], P('section', 'lat', 'lon'), may hold values from -6 to 6
- incoming_grad: bfloat16 [2, 48, 768, 512], P('section', 'lat', 'lon'), may hold values from -6 to 6
- saved_coeffs: bfloat16 [2, 2, 384, 384, 512], P('section', None, None, 'lat', 'lon'), may hold values from -6 to 6
- filter_weights: float32 [2, 2, 384, 512], P('section', None, None, 'lon'), may hold values from -6 to 6
- up_weight: bfloat16 [2, 512, 512], P('section'), may hold values from -0.25 to 0.25
- down_weight: bfloat16 [2, 512, 512], P('section'), may hold values from -0.25 to 0.25
- latitude_maps: bfloat16 [384, 384, 48], P('lat'), may hold values from -0.3125 to 0.3125
Outputs:
- handed_grad: bfloat16 [2, 48, 768, 512], P('section', 'lat', 'lon')
- filter_grad: float32 [2, 2, 384, 512], P('section', None, 'lat', 'lon')
- up_grad: float32 [2, 512, 512], P('section', ('lat', 'lon'))
- down_grad: float32 [2, 512, 512], P('section', ('lat', 'lon'))
All inputs are finite; a program needn't handle non-finite values.
Results may differ from a plain program's by a relative error of at most 0.0085.
Values may be sent and summed in bfloat16 or wider, within the bound.
A program may use at most 256 MiB of HBM per device.

v0:
```python
import math

import jax
import jax.numpy as jnp
from jax import lax
from jax.sharding import PartitionSpec as P

MODES = 384


def shifted(block, axis, distance):
    devices = range(lax.axis_size(axis))
    route = [((i - distance) % len(devices), i) for i in devices]
    return lax.ppermute(block, axis, route)


def transform_tables(offset, length, period, orders_kept):
    positions = offset + jnp.arange(length, dtype=jnp.int32)
    orders = jnp.arange(orders_kept, dtype=jnp.int32)
    phases = positions[:, None] * orders[None, :] % period
    angles = phases.astype(jnp.float32) * (2.0 * math.pi / period)
    factor = 1.0 / math.sqrt(period)
    cosine = jnp.cos(angles) * factor
    sine_part = jnp.sin(angles) * factor
    doubled = jnp.where(orders == 0, 1.0, 2.0).astype(jnp.float32)[None, :]
    synthesis = jnp.stack([cosine * doubled, -sine_part * doubled]).astype(jnp.bfloat16)
    analysis = jnp.stack([cosine, -sine_part]).astype(jnp.bfloat16)
    return (synthesis, analysis)


def gelu_pair(pre_active):
    normal_cdf = 0.5 * (1.0 + lax.erf(pre_active * (1.0 / math.sqrt(2.0))))
    density = jnp.exp(-0.5 * pre_active * pre_active) * (1.0 / math.sqrt(2.0 * math.pi))
    return (pre_active * normal_cdf, normal_cdf + pre_active * density)


def shards(
    block_hidden, incoming_grad, saved_coeffs, filter_weights, up_weight, down_weight, latitude_maps
):
    band_rows = block_hidden.shape[1]
    slab_width = block_hidden.shape[2]
    embed = block_hidden.shape[3]
    token_rows = block_hidden[0].reshape(band_rows * slab_width, embed)
    grad_rows = incoming_grad[0].reshape(band_rows * slab_width, embed)
    up_matrix = up_weight[0]
    down_matrix = down_weight[0]
    pre_active = jnp.dot(token_rows, up_matrix, preferred_element_type=jnp.float32)
    activation, slopes = gelu_pair(pre_active)
    activated = activation.astype(jnp.bfloat16)
    carried = lax.dot_general(
        grad_rows, down_matrix, (((1,), (1,)), ((), ())), preferred_element_type=jnp.float32
    )
    grad_pre = (carried * slopes).astype(jnp.bfloat16)
    down_terms = lax.dot_general(
        activated, grad_rows, (((0,), (0,)), ((), ())), preferred_element_type=jnp.float32
    )
    up_terms = lax.dot_general(
        token_rows, grad_pre, (((0,), (0,)), ((), ())), preferred_element_type=jnp.float32
    )
    back_rows = lax.dot_general(
        grad_pre, up_matrix, (((1,), (1,)), ((), ())), preferred_element_type=jnp.float32
    )
    grad_hidden = (grad_rows.astype(jnp.float32) + back_rows).astype(jnp.bfloat16)
    grad_grid = grad_hidden.reshape(band_rows, slab_width, embed)
    group_count = lax.axis_size(("lat", "lon"))
    group_index = lax.axis_index(("lat", "lon"))
    up_total, down_total = lax.psum((up_terms, down_terms), ("lat", "lon"))
    up_share = up_total.shape[0] // group_count
    down_share = down_total.shape[0] // group_count
    up_grad = lax.dynamic_slice_in_dim(up_total, group_index * up_share, up_share, 0)
    down_grad = lax.dynamic_slice_in_dim(down_total, group_index * down_share, down_share, 0)
    period = slab_width * lax.axis_size("lon")
    synthesis, analysis = transform_tables(
        lax.axis_index("lon") * slab_width, slab_width, period, MODES
    )
    partial_terms = jnp.einsum(
        "tkc,rkm->rtmc", grad_grid, synthesis, preferred_element_type=jnp.float32
    )
    spectrum = lax.psum_scatter(partial_terms, "lon", scatter_dimension=3, tiled=True).astype(
        jnp.bfloat16
    )
    order_major = lax.all_to_all(spectrum, "lat", split_axis=2, concat_axis=1, tiled=True)
    degree_grad = jnp.einsum(
        "mlt,rtmc->rlmc", latitude_maps, order_major, preferred_element_type=jnp.float32
    )
    coeffs_local = saved_coeffs[0].astype(jnp.float32)
    filter_terms = jnp.stack(
        [
            jnp.sum(degree_grad[0] * coeffs_local[0] + degree_grad[1] * coeffs_local[1], axis=1),
            jnp.sum(degree_grad[1] * coeffs_local[0] - degree_grad[0] * coeffs_local[1], axis=1),
        ]
    )
    weight_real = filter_weights[0, 0][:, None, :]
    weight_imag = filter_weights[0, 1][:, None, :]
    coef_grad = jnp.stack(
        [
            weight_real * degree_grad[0] + weight_imag * degree_grad[1],
            weight_real * degree_grad[1] - weight_imag * degree_grad[0],
        ]
    ).astype(jnp.bfloat16)
    band_grad = jnp.einsum(
        "mlt,rlmc->rtmc", latitude_maps, coef_grad, preferred_element_type=jnp.float32
    ).astype(jnp.bfloat16)
    band_major = lax.all_to_all(band_grad, "lat", split_axis=1, concat_axis=2, tiled=True)
    filter_total = lax.psum(filter_terms, "lat")
    degree_share = filter_total.shape[1] // lax.axis_size("lat")
    filter_grad = lax.dynamic_slice_in_dim(
        filter_total, lax.axis_index("lat") * degree_share, degree_share, 1
    )
    grid_back = jnp.einsum(
        "rtmc,rkm->tkc",
        lax.all_gather(band_major, "lon", axis=3, tiled=True),
        analysis,
        preferred_element_type=jnp.float32,
    ).astype(jnp.bfloat16)
    passed = (grad_grid.astype(jnp.float32) + grid_back.astype(jnp.float32)).astype(jnp.bfloat16)
    handed_grad = shifted(passed[None], "section", 1)
    return (handed_grad, filter_grad[None], up_grad[None], down_grad[None])


def solution(mesh):
    in_specs = (
        P("section", "lat", "lon", None),
        P("section", "lat", "lon", None),
        P("section", None, None, "lat", "lon"),
        P("section", None, None, "lon"),
        P("section", None, None),
        P("section", None, None),
        P("lat", None, None),
    )
    out_specs = (
        P("section", "lat", "lon", None),
        P("section", None, "lat", "lon"),
        P("section", ("lat", "lon"), None),
        P("section", ("lat", "lon"), None),
    )
    return jax.shard_map(shards, mesh=mesh, in_specs=in_specs, out_specs=out_specs, check_vma=False)
```

profile of v0, /device:TPU:0, one launch (start us, length us, event | category | flops | bytes accessed | tf_op | source)
XLA Modules:
  0.0 447.3 jit_solution(3697079684727871473)
XLA Ops:
  8.0 0.0 copy-start
  8.0 0.0 reduce-scatter.2.cloned.1.call-start
  8.1 1.6 copy-done
  9.7 2.6 fusion.30
  12.3 3.0 fusion.9
  15.3 1.5 fusion.10
  16.8 3.4 multiply_convert_fusion.4
  20.2 5.1 %convolution_bitcast_fusion.1 = f32[2,6,384,512]{3,2,1,0:T(8,128)} fusion(bf16[6,384,512,1]{2,1,0,3:T(8,128)(2,1)S(1)} %bitcast.95, bf16[1,384,384]{1,2,0:T(8,128)(2,1)S(1)} %get-tuple-element.17, bf16[1,384,384]{1,2,0:T(8,128)(2,1)S(1)} %get-tuple-element.15), kind=kOutput, calls=%fused_computation.25 | convolution fusion | flops 1813118976 | bytes 12386304 | tf_op jit(solution)/shard_map/tkc,rkm->rtmc/dot_general | solution.py:76
  25.3 0.0 reduce-scatter.2.cloned.1.call-update
  25.4 20.6 %reduce-scatter.2.cloned.1.call-done = f32[2,6,384,256]{3,2,1,0:T(8,128)} async-done(((f32[2,6,384,512]{3,2,1,0:T(8,128)}), f32[2,6,384,256]{3,2,1,0:T(8,128)}) %reduce-scatter.2.cloned.1.call-update) | async-done | bytes 4718608 | tf_op jit(solution)/shard_map/reduce_scatter | solution.py:79
  46.0 2.6 convert_element_type.71
  48.6 3.9 copy.54
  52.5 5.9 %all-to-all-start = ((bf16[2,6,384,256]{3,0,1,2:T(2,128)(2,1)}), bf16[2,6,384,256]{3,0,1,2:T(2,128)(2,1)}, u32[]{:S(2)}, u32[]{:S(2)}) async-start(bf16[2,6,384,256]{3,0,1,2:T(2,128)(2,1)} %copy.54), calls=%async_computation.1 | async-start | bytes 4718592 | tf_op jit(solution)/shard_map/all_to_all | solution.py:82
  58.4 0.2 all-gather.2.cloned.1.call-start
  58.6 1.2 slice_bitcast_fusion.3
  59.8 0.2 copy.53
  60.0 0.2 copy.58
  60.1 25.0 %copy.64 = bf16[1,2,384,48,256]{2,4,3,1,0:T(8,128)(2,1)} copy(bf16[1,2,384,48,256]{4,3,2,1,0:T(8,128)(2,1)} %param.9) | data formatting | bytes 37748736 | tf_op args[2]
  85.1 20.9 %convert_element_type.78 = f32[1,2,384,48,256]{2,4,3,1,0:T(8,128)} convert(bf16[1,2,384,48,256]{2,4,3,1,0:T(8,128)(2,1)} %copy.64) | non-fusion elementwise | flops 9437184 | bytes 56623104 | tf_op jit(solution)/shard_map/convert_element_type | solution.py:86
  106.0 6.7 %all-to-all-done = bf16[2,6,384,256]{3,0,1,2:T(2,128)(2,1)} async-done(((bf16[2,6,384,256]{3,0,1,2:T(2,128)(2,1)}), bf16[2,6,384,256]{3,0,1,2:T(2,128)(2,1)}, u32[]{:S(2)}, u32[]{:S(2)}) %all-to-all-start) | async-done | bytes 2359328 | tf_op jit(solution)/shard_map/all_to_all | solution.py:82
  112.7 2.1 copy.55
  114.8 0.2 copy.56
  115.1 14.7 %convolution_bitcast_fusion = f32[2,384,48,256]{1,3,0,2:T(8,128)} fusion(bf16[2,48,48,256]{3,2,1,0:T(8,128)(2,1)S(1)} %bitcast.91, bf16[48,384,48]{1,2,0:T(8,128)(2,1)S(1)} %copy-done.3), kind=kOutput, calls=%fused_computation.10 | convolution fusion | flops 905969664 | bytes 41877504 | tf_op jit(solution)/shard_map/mlt,rtmc->rlmc/dot_general | solution.py:83
  129.8 33.3 %add_reduce_fusion = (f32[384,256]{0,1:T(8,128)S(1)}, f32[384,256]{0,1:T(8,128)}, bf16[1,384,48,256]{1,3,0,2:T(8,128)(2,1)}, bf16[1,384,48,256]{1,3,0,2:T(8,128)(2,1)}) fusion(f32[1,2,384,48,256]{2,4,3,1,0:T(8,128)} %convert_element_type.78, f32[2,384,48,256]{1,3,0,2:T(8,128)} %convolution_bitcast_fusion, f32[384,256]{0,1:T(8,128)S(1)} %copy.58, ...), kind=kLoop, calls=%fused_computation.7 | loop fusion | flops 75300864 | bytes 95944704 | tf_op jit(solution)/shard_map/reduce_sum | solution.py:89
  163.1 10.6 %convert_bitcast_fusion = bf16[2,48,48,256]{3,1,0,2:T(8,128)(2,1)S(1)} fusion(bf16[1,384,48,256]{1,3,0,2:T(8,128)(2,1)} %get-tuple-element.10, bf16[1,384,48,256]{1,3,0,2:T(8,128)(2,1)} %get-tuple-element.11, bf16[48,384,48]{1,2,0:T(8,128)(2,1)S(1)} %copy-done.3), kind=kOutput, calls=%fused_computation.29 | convolution fusion | flops 916586496 | bytes 23003136 | tf_op jit(solution)/shard_map/mlt,rlmc->rtmc/dot_general | solution.py:101
  173.7 2.6 copy.60
  176.3 57.4 %all_to_all.36 = bf16[2,48,48,256]{3,0,2,1:T(2,128)(2,1)S(1)} all-to-all(bf16[2,48,48,256]{3,0,2,1:T(2,128)(2,1)S(1)} %copy.60), channel_id=1, replica_groups=mesh['section'=2,'lat'=8,'lon'=2] {'lat'}, dimensions={1} | all-to-all | bytes 4718592 | tf_op jit(solution)/shard_map/all_to_all | solution.py:104
  233.7 0.4 copy.61
  234.1 1.6 copy.62
  235.7 0.0 all-gather.2.cloned.1.call-update
  235.8 0.3 all-reduce.6.cloned.1.call-start
  236.0 5.5 %fusion.11 = f32[512,512]{1,0:T(8,128)} fusion(bf16[2304,512]{1,0:T(8,128)(2,1)} %bitcast.101, f32[2304,512]{1,0:T(8,128)} %copy-done.1), kind=kOutput, calls=%fused_computation.26 | convolution fusion | flops 1213857792 | bytes 8126464 | tf_op jit(solution)/shard_map/dot_general | solution.py:54
  241.6 7.1 %all-gather.2.cloned.1.call-done = bf16[2,6,384,512]{3,2,0,1:T(8,128)(2,1)} async-done(((bf16[2,6,384,256]{3,2,0,1:T(8,128)(2,1)}), bf16[2,6,384,512]{3,2,0,1:T(8,128)(2,1)}) %all-gather.2.cloned.1.call-update) | async-done | bytes 4718608 | tf_op jit(solution)/shard_map/all_gather | solution.py:112
  248.7 6.7 %fusion.12 = bf16[1,6,384,512]{3,2,1,0:T(8,128)(2,1)} fusion(bf16[6,384,512]{2,1,0:T(8,128)(2,1)} %bitcast.96, bf16[2,6,384,512]{3,2,0,1:T(8,128)(2,1)} %all-gather.2.cloned.1.call-done, bf16[1,384,384]{1,2,0:T(8,128)(2,1)S(1)} %copy-done.7, bf16[1,384,384]{1,2,0:T(8,128)(2,1)S(1)} %copy-done.6), kind=kOutput, calls=%fused_computation.27 | convolution fusion | flops 1819017216 | bytes 10027008 | tf_op jit(solution)/shard_map/rtmc,rkm->tkc/dot_general | solution.py:110
  255.3 1.8 collective-permute-start
  257.1 2.4 convolution_bitcast_fusion.2
  259.5 0.0 all-reduce.6.cloned.1.call-update
  259.6 0.0 all-reduce.4.cloned.1.call-start
  259.6 1.0 pad_maximum_fusion
  260.6 0.0 all-reduce.4.cloned.1.call-update
  260.6 96.6 %all-reduce.6.cloned.1.call-done = (f32[512,512]{0,1:T(8,128)}, f32[512,512]{1,0:T(8,128)}) async-done(((f32[512,512]{0,1:T(8,128)}, f32[512,512]{1,0:T(8,128)}), (f32[512,512]{0,1:T(8,128)}, f32[512,512]{1,0:T(8,128)})) %all-reduce.6.cloned.1.call-update) | async-done | bytes 2097168 | tf_op jit(solution)/shard_map/psum | solution.py:67
  357.2 1.1 constant_dynamic-slice_fusion
  358.3 0.7 copy.66
  359.0 1.5 dynamic-slice_bitcast_fusion
  360.5 74.0 %all-reduce.4.cloned.1.call-done = f32[2,384,256]{1,2,0:T(8,128)} async-done(((f32[2,384,256]{1,2,0:T(8,128)}), f32[2,384,256]{1,2,0:T(8,128)}) %all-reduce.4.cloned.1.call-update) | async-done | bytes 786448 | tf_op jit(solution)/shard_map/psum | solution.py:105
  434.6 1.2 constant_dynamic-slice_fusion.1
  435.7 0.8 copy.65
  436.5 3.4 copy.79
  (25 shorter events, 0.1 us)
Async XLA Ops:
  8.0 1.7 copy-start
  8.0 38.0 %reduce-scatter.2.cloned.1.call-start = ((), (), s32[]{:S(2)}) async-start(), calls=%async_computation.3 | async-start | bytes 14155776 | tf_op jit(solution)/shard_map/reduce_scatter | solution.py:79
  9.7 2.6 copy-start.8
  9.7 2.6 copy-start.9
  12.3 3.0 copy-start.1
  12.3 3.0 copy-start.5
  15.3 1.5 copy-start.10
  16.8 3.4 copy-start.2
  52.5 60.2 %all-to-all-start = ((bf16[2,6,384,256]{3,0,1,2:T(2,128)(2,1)}), bf16[2,6,384,256]{3,0,1,2:T(2,128)(2,1)}, u32[]{:S(2)}, u32[]{:S(2)}) async-start(bf16[2,6,384,256]{3,0,1,2:T(2,128)(2,1)} %copy.54), calls=%async_computation.1 | async-start | bytes 4718592 | tf_op jit(solution)/shard_map/all_to_all | solution.py:82
  58.4 190.3 %all-gather.2.cloned.1.call-start = ((), (), s32[]{:S(2)}) async-start(), calls=%async_computation.4 | async-start | bytes 7077888 | tf_op jit(solution)/shard_map/all_gather | solution.py:112
  112.7 2.4 copy-start.3
  235.7 12.9 %copy-start.6 = (bf16[1,384,384]{1,2,0:T(8,128)(2,1)S(1)}, bf16[1,384,384]{1,2,0:T(8,128)(2,1)}, u32[]{:S(2)}) copy-start(bf16[1,384,384]{1,2,0:T(8,128)(2,1)} %get-tuple-element.14) | copy-start | bytes 884740
  235.8 12.9 %copy-start.7 = (bf16[1,384,384]{1,2,0:T(8,128)(2,1)S(1)}, bf16[1,384,384]{1,2,0:T(8,128)(2,1)}, u32[]{:S(2)}) copy-start(bf16[1,384,384]{1,2,0:T(8,128)(2,1)} %get-tuple-element.16) | copy-start | bytes 884740
  235.8 121.5 %all-reduce.6.cloned.1.call-start = ((), (), s32[]{:S(2)}) async-start(), calls=%async_computation.6 | async-start | bytes 4194304 | tf_op jit(solution)/shard_map/psum | solution.py:67
  248.7 8.4 %copy-start.11 = (bf16[2304,512]{1,0:T(8,128)(2,1)S(1)}, bf16[2304,512]{1,0:T(8,128)(2,1)}, u32[]{:S(2)}) copy-start(bf16[2304,512]{1,0:T(8,128)(2,1)} %copy-done.10) | copy-start | bytes 7077892
  255.3 4.3 copy-start.4
  255.3 181.2 %collective-permute-start = (bf16[1,6,384,512]{3,2,1,0:T(8,128)(2,1)}, bf16[1,6,384,512]{3,2,1,0:T(8,128)(2,1)}, u32[]{:S(2)}, u32[]{:S(2)}) collective-permute-start(bf16[1,6,384,512]{3,2,1,0:T(8,128)(2,1)} %fusion.12), channel_id=1, source_target_pairs={{16,0},{0,16},{17,1},{1,17},{18,2},{2,18},{19,3},{3,19},{20,4},{4,... | collective-permute-start | bytes 7077896 | tf_op jit(solution)/shard_map/ppermute | solution.py:14
  259.6 175.0 %all-reduce.4.cloned.1.call-start = ((), (), s32[]{:S(2)}) async-start(), calls=%async_computation.5 | async-start | bytes 1572864 | tf_op jit(solution)/shard_map/psum | solution.py:105
Sparse Core Ops, SparseCore 0:
  25.5 20.4 reduce-scatter.1
  235.9 12.7 all-gather.1
Sparse Core Ops, SparseCore 1:
  259.6 97.5 all-reduce.5
  360.9 73.6 all-reduce.3
where the time goes:
time: 448 us; the launch traced here: 447 us
  waiting for transfers between devices  205 us (46%)
  other arithmetic  61.2 us (14%)
  blocking collectives  57.4 us (13%)
  matrix products  52.1 us (12%)
  local copies, waits for them, and re-layouts  47.5 us (11%)
  between operations  15.7 us (4%)
  starting transfers between devices  8.25 us (2%)
    psum x1, waiting for transfers between devices, shards(): up_total, down_total = lax.psum((up_terms, down_terms), ('lat', 'lon'))  96.6 us
    psum x1, waiting for transfers between devices, shards(): filter_total = lax.psum(filter_terms, 'lat')  74 us
    all_to_all x1, blocking collectives, shards(): lax.all_to_all(band_grad, 'lat', split_axis=1, concat_axis=2, tiled=True)  57.4 us
    reduce_sum x1, other arithmetic, shards(): jnp.sum(degree_grad[0] * coeffs_local[0] + degree_grad[1] * coeffs_local[...  33.3 us
    unnamed x26, local copies, waits for them, and re-layouts  30 us
    convert_element_type x1, other arithmetic, shards(): coeffs_local = saved_coeffs[0].astype(jnp.float32)  20.9 us
    reduce_scatter x1, waiting for transfers between devices, shards(): lax.psum_scatter(partial_terms, 'lon', scatter_dimension=3, tiled=True)  20.6 us
    dot_general x1, matrix products, shards(): jnp.einsum('mlt,rtmc->rlmc', latitude_maps, order_major, preferred_elemen...  14.7 us
  transfers between devices with their start and end apart: 6, of which 5 were waited for; matrix products, arithmetic and copies ran while one was open for 14% of the time, Pallas kernels for 0%

commit v1 on v0

--- a/solution.py
+++ b/solution.py
@@ -1,8 +1,11 @@
+import functools
 import math
 
 import jax
 import jax.numpy as jnp
 from jax import lax
+from jax.experimental import pallas as pl
+from jax.experimental.pallas import tpu as pltpu
 from jax.sharding import PartitionSpec as P
 
 MODES = 384
@@ -32,6 +35,142 @@
     normal_cdf = 0.5 * (1.0 + lax.erf(pre_active * (1.0 / math.sqrt(2.0))))
     density = jnp.exp(-0.5 * pre_active * pre_active) * (1.0 / math.sqrt(2.0 * math.pi))
     return (pre_active * normal_cdf, normal_cdf + pre_active * density)
+
+GROUP = 16
+
+
+def swap_matrix():
+    row = lax.broadcasted_iota(jnp.int32, (GROUP * GROUP, GROUP * GROUP), 0)
+    column = lax.broadcasted_iota(jnp.int32, (GROUP * GROUP, GROUP * GROUP), 1)
+    partner = row % GROUP * GROUP + row // GROUP
+    return jnp.where(partner == column, 1.0, 0.0).astype(jnp.bfloat16)
+
+
+def swapped(matrix, block):
+    flat = block.reshape(GROUP * GROUP, block.shape[2])
+    turned = jnp.dot(matrix, flat, preferred_element_type=jnp.float32)
+    return turned.astype(jnp.bfloat16).reshape(block.shape)
+
+
+def middle_group(
+    first, x_ref, s_ref, w_ref, map_ref, filter_ref, out_ref, swap_ref, x_major, s_major, out_major
+):
+    lats, width = x_ref.shape[1], x_ref.shape[3]
+    degrees = s_ref.shape[1]
+    matrix = swap_ref[...]
+    for part in range(2):
+        lanes = slice(part * width, (part + 1) * width)
+        for piece in range(lats // GROUP):
+            rows = slice(piece * GROUP, (piece + 1) * GROUP)
+            x_major[:, rows, lanes] = swapped(matrix, x_ref[part, rows])
+
+        @pl.loop(0, degrees // GROUP)
+        def _(piece):
+            rows = pl.ds(pl.multiple_of(piece * GROUP, GROUP), GROUP)
+            s_major[:, rows, lanes] = swapped(matrix, s_ref[part, rows])
+
+    @pl.when(first)
+    def _():
+        filter_ref[...] = jnp.zeros_like(filter_ref)
+
+    chunk = 128
+
+    @pl.loop(0, GROUP)
+    def _(order):
+        band = jnp.zeros((lats, 2 * width), jnp.float32)
+        bands = x_major[order]
+        for start in range(0, degrees, chunk):
+            rows = slice(start, start + chunk)
+            maps = map_ref[order, :, rows]
+            degree = lax.dot_general(
+                maps, bands, (((0,), (0,)), ((), ())), preferred_element_type=jnp.float32
+            )
+            real, imag = degree[:, :width], degree[:, width:]
+            saved_real = s_major[order, rows, :width].astype(jnp.float32)
+            saved_imag = s_major[order, rows, width:].astype(jnp.float32)
+            filter_ref[0, rows] += real * saved_real + imag * saved_imag
+            filter_ref[1, rows] += imag * saved_real - real * saved_imag
+            weight_real, weight_imag = w_ref[0, rows], w_ref[1, rows]
+            coefs = jnp.concatenate(
+                [
+                    (weight_real * real + weight_imag * imag).astype(jnp.bfloat16),
+                    (weight_real * imag - weight_imag * real).astype(jnp.bfloat16),
+                ],
+                axis=1,
+            )
+            band = band + jnp.dot(maps, coefs, preferred_element_type=jnp.float32)
+        out_major[order] = band.astype(jnp.bfloat16)
+
+    for part in range(2):
+        lanes = slice(part * width, (part + 1) * width)
+        for piece in range(lats // GROUP):
+            rows = slice(piece * GROUP, (piece + 1) * GROUP)
+            out_ref[part, rows] = swapped(matrix, out_major[:, rows, lanes])
+
+
+def middle_kernel(swap_ref, x_ref, s_ref, w_ref, map_ref, filter_ref, out_ref, *scratch):
+    middle_group(
+        pl.program_id(0) == 0, x_ref, s_ref, w_ref, map_ref, filter_ref, out_ref, swap_ref, *scratch
+    )
+
+
+def middle(order_major, saved, weights, maps):
+    _, lats, orders, width = order_major.shape
+    degrees = saved.shape[1]
+    return pl.pallas_call(
+        middle_kernel,
+        grid=(orders // GROUP,),
+        in_specs=[
+            pl.BlockSpec((GROUP * GROUP, GROUP * GROUP), lambda i: (0, 0)),
+            pl.BlockSpec((2, lats, GROUP, width), lambda i: (0, 0, i, 0)),
+            pl.BlockSpec((2, degrees, GROUP, width), lambda i: (0, 0, i, 0)),
+            pl.BlockSpec((2, degrees, width), lambda i: (0, 0, 0)),
+            pl.BlockSpec((GROUP, lats, degrees), lambda i: (i, 0, 0)),
+        ],
+        out_specs=[
+            pl.BlockSpec((2, degrees, width), lambda i: (0, 0, 0)),
+            pl.BlockSpec((2, lats, GROUP, width), lambda i: (0, 0, i, 0)),
+        ],
+        out_shape=[
+            jax.ShapeDtypeStruct((2, degrees, width), jnp.float32),
+            jax.ShapeDtypeStruct(order_major.shape, jnp.bfloat16),
+        ],
+        scratch_shapes=[
+            pltpu.VMEM((GROUP, lats, 2 * width), jnp.bfloat16),
+            pltpu.VMEM((GROUP, degrees, 2 * width), jnp.bfloat16),
+            pltpu.VMEM((GROUP, lats, 2 * width), jnp.bfloat16),
+        ],
+        compiler_params=pltpu.CompilerParams(vmem_limit_bytes=48 << 20),
+        cost_estimate=pl.CostEstimate(
+            flops=8 * lats * orders * degrees * width,
+            bytes_accessed=saved.size * 2 + order_major.size * 4,
+            transcendentals=0,
+        ),
+    )(swap_matrix(), order_major, saved, weights, jnp.swapaxes(maps, 1, 2))
+
+
+def middle_plain(order_major, saved, weights, maps):
+    degree_grad = jnp.einsum(
+        "mlt,rtmc->rlmc", maps, order_major, preferred_element_type=jnp.float32
+    )
+    saved = saved.astype(jnp.float32)
+    filter_terms = jnp.stack(
+        [
+            jnp.sum(degree_grad[0] * saved[0] + degree_grad[1] * saved[1], axis=1),
+            jnp.sum(degree_grad[1] * saved[0] - degree_grad[0] * saved[1], axis=1),
+        ]
+    )
+    real, imag = weights[0][:, None, :], weights[1][:, None, :]
+    coef_grad = jnp.stack(
+        [
+            real * degree_grad[0] + imag * degree_grad[1],
+            real * degree_grad[1] - imag * degree_grad[0],
+        ]
+    ).astype(jnp.bfloat16)
+    band_grad = jnp.einsum(
+        "mlt,rlmc->rtmc", maps, coef_grad, preferred_element_type=jnp.float32
+    ).astype(jnp.bfloat16)
+    return filter_terms, band_grad
 
 
 def shards(
@@ -63,56 +202,53 @@
     grad_hidden = (grad_rows.astype(jnp.float32) + back_rows).astype(jnp.bfloat16)
     grad_grid = grad_hidden.reshape(band_rows, slab_width, embed)
     group_count = lax.axis_size(("lat", "lon"))
-    group_index = lax.axis_index(("lat", "lon"))
-    up_total, down_total = lax.psum((up_terms, down_terms), ("lat", "lon"))
-    up_share = up_total.shape[0] // group_count
-    down_share = down_total.shape[0] // group_count
-    up_grad = lax.dynamic_slice_in_dim(up_total, group_index * up_share, up_share, 0)
-    down_grad = lax.dynamic_slice_in_dim(down_total, group_index * down_share, down_share, 0)
-    period = slab_width * lax.axis_size("lon")
-    synthesis, analysis = transform_tables(
-        lax.axis_index("lon") * slab_width, slab_width, period, MODES
-    )
-    partial_terms = jnp.einsum(
-        "tkc,rkm->rtmc", grad_grid, synthesis, preferred_element_type=jnp.float32
-    )
-    spectrum = lax.psum_scatter(partial_terms, "lon", scatter_dimension=3, tiled=True).astype(
-        jnp.bfloat16
-    )
-    order_major = lax.all_to_all(spectrum, "lat", split_axis=2, concat_axis=1, tiled=True)
-    degree_grad = jnp.einsum(
-        "mlt,rtmc->rlmc", latitude_maps, order_major, preferred_element_type=jnp.float32
-    )
-    coeffs_local = saved_coeffs[0].astype(jnp.float32)
-    filter_terms = jnp.stack(
-        [
-            jnp.sum(degree_grad[0] * coeffs_local[0] + degree_grad[1] * coeffs_local[1], axis=1),
-            jnp.sum(degree_grad[1] * coeffs_local[0] - degree_grad[0] * coeffs_local[1], axis=1),
-        ]
-    )
-    weight_real = filter_weights[0, 0][:, None, :]
-    weight_imag = filter_weights[0, 1][:, None, :]
-    coef_grad = jnp.stack(
-        [
-            weight_real * degree_grad[0] + weight_imag * degree_grad[1],
-            weight_real * degree_grad[1] - weight_imag * degree_grad[0],
-        ]
-    ).astype(jnp.bfloat16)
-    band_grad = jnp.einsum(
-        "mlt,rlmc->rtmc", latitude_maps, coef_grad, preferred_element_type=jnp.float32
-    ).astype(jnp.bfloat16)
-    band_major = lax.all_to_all(band_grad, "lat", split_axis=1, concat_axis=2, tiled=True)
-    filter_total = lax.psum(filter_terms, "lat")
-    degree_share = filter_total.shape[1] // lax.axis_size("lat")
-    filter_grad = lax.dynamic_slice_in_dim(
-        filter_total, lax.axis_index("lat") * degree_share, degree_share, 1
-    )
-    grid_back = jnp.einsum(
-        "rtmc,rkm->tkc",
-        lax.all_gather(band_major, "lon", axis=3, tiled=True),
-        analysis,
+    lat_count = lax.axis_size("lat")
+    lon_index = lax.axis_index("lon")
+    half = embed // 2
+    period = slab_width * 2
+    synthesis, analysis = transform_tables(0, slab_width * 2, period, MODES)
+    other = jnp.where(lon_index == 0, grad_grid[..., half:], grad_grid[..., :half])
+    own = jnp.where(lon_index == 0, grad_grid[..., :half], grad_grid[..., half:])
+    theirs = shifted(other, "lon", 1)
+    own_start = lon_index * slab_width
+    their_start = (1 - lon_index) * slab_width
+    own_table = lax.dynamic_slice_in_dim(synthesis, own_start, slab_width, 1)
+    their_table = lax.dynamic_slice_in_dim(synthesis, their_start, slab_width, 1)
+    spectrum = jnp.einsum(
+        "tkc,rkm->rtmc",
+        jnp.concatenate([own, theirs], axis=1),
+        jnp.concatenate([own_table, their_table], axis=1),
         preferred_element_type=jnp.float32,
     ).astype(jnp.bfloat16)
+    order_major = lax.all_to_all(spectrum, "lat", split_axis=2, concat_axis=1, tiled=True)
+    mixer_terms = jnp.stack([up_terms, down_terms]).astype(jnp.bfloat16)
+    mixer_terms = mixer_terms.reshape(2, group_count, -1, up_terms.shape[1])
+    mixer_parts = lax.all_to_all(mixer_terms, ("lat", "lon"), split_axis=1, concat_axis=1, tiled=True)
+    up_grad, down_grad = jnp.sum(mixer_parts.astype(jnp.float32), axis=1)
+    fits = order_major.shape[2] % GROUP == 0 and order_major.shape[1] <= 64
+    filter_terms, band_grad = (middle if fits else middle_plain)(
+        order_major, saved_coeffs[0], filter_weights[0], latitude_maps
+    )
+    band_major = lax.all_to_all(band_grad, "lat", split_axis=1, concat_axis=2, tiled=True)
+    filter_terms = filter_terms.reshape(2, lat_count, -1, half).astype(jnp.bfloat16)
+    filter_parts = lax.all_to_all(filter_terms, "lat", split_axis=1, concat_axis=1, tiled=True)
+    filter_grad = jnp.sum(filter_parts.astype(jnp.float32), axis=1)
+
+    def back(start):
+        table = lax.dynamic_slice_in_dim(analysis, start, slab_width, 1)
+        return jnp.einsum(
+            "rtmc,rkm->tkc", band_major, table, preferred_element_type=jnp.float32
+        ).astype(jnp.bfloat16)
+
+    their_back = shifted(back(their_start), "lon", 1)
+    own_back = back(own_start)
+    grid_back = jnp.concatenate(
+        [
+            jnp.where(lon_index == 0, own_back, their_back),
+            jnp.where(lon_index == 0, their_back, own_back),
+        ],
+        axis=2,
+    )
     passed = (grad_grid.astype(jnp.float32) + grid_back.astype(jnp.float32)).astype(jnp.bfloat16)
     handed_grad = shifted(passed[None], "section", 1)
     return (handed_grad, filter_grad[None], up_grad[None], down_grad[None])

time: 448 us -> 312 us (0.70)
  Pallas kernels: 0 us -> 65.9 us
  waiting for transfers between devices: 205 us -> 144 us
  blocking collectives: 57.4 us -> 0 us
  other arithmetic: 61.2 us -> 23.1 us
  matrix products: 52.1 us -> 24.6 us
  local copies, waits for them, and re-layouts: 47.5 us -> 28.9 us
  starting transfers between devices: 8.25 us -> 24.2 us
  between operations: 15.7 us -> 0.84 us
    psum x2 -> x0, waiting for transfers between devices: 171 us -> none  [the longest x1 96.6 us: shards(): up_total, down_total = lax.psum((up_terms, down_terms), ('lat', 'lon'))]
    all_to_all x0 -> x3, waiting for transfers between devices: none -> 72.7 us  [the longest x1 47.5 us: shards(): lax.all_to_all(band_grad, 'lat', split_axis=1, concat_axis=2, tiled=True)]
    pallas_call x0 -> x1, Pallas kernels: none -> 65.9 us  [middle(): pl.pallas_call(middle_kernel, grid=(orders // GROUP,), in_specs=[pl.Block...]
    all_to_all x1 -> x0, blocking collectives: 57.4 us -> none  [shards(): lax.all_to_all(band_grad, 'lat', split_axis=1, concat_axis=2, tiled=True)]
    all_to_all x1, waiting for transfers between devices: 6.66 us -> 54.3 us  [shards(): lax.all_to_all(spectrum, 'lat', split_axis=2, concat_axis=1, tiled=True)]
    reduce_sum x1 -> x2, other arithmetic: 33.3 us -> 2.07 us  [the longest x1 1.38 us: shards(): up_grad, down_grad = jnp.sum(mixer_parts.astype(jnp.float32), axis=1)]
    dot_general x4 -> x3, matrix products: 37.1 us -> 8.9 us  [the longest x2 5.64 us: back(): jnp.einsum('rtmc,rkm->tkc', band_major, table, preferred_element_type=jnp...]
    unnamed x26 -> x29, local copies, waits for them, and re-layouts: 30 us -> 8.88 us
  transfers between devices with their start and end apart: 6 -> 7, of which waited for: 5 -> 5; matrix products, arithmetic and copies ran while one was open for 14% -> 9% of each run, Pallas kernels for 0% -> 0%
where the time goes in v1:
time: 312 us; the launch traced here: 311 us
  waiting for transfers between devices  144 us (46%)
  Pallas kernels  65.9 us (21%)
  local copies, waits for them, and re-layouts  28.9 us (9%)
  matrix products  24.6 us (8%)
  starting transfers between devices  24.2 us (8%)
  other arithmetic  23.1 us (7%)
    pallas_call x1, Pallas kernels, middle(): pl.pallas_call(middle_kernel, grid=(orders // GROUP,), in_specs=[pl.Block...  65.9 us
    all_to_all x1, waiting for transfers between devices, shards(): lax.all_to_all(spectrum, 'lat', split_axis=2, concat_axis=1, tiled=True)  54.3 us
    all_to_all x1, waiting for transfers between devices, shards(): lax.all_to_all(band_grad, 'lat', split_axis=1, concat_axis=2, tiled=True)  47.5 us
    ppermute x3, waiting for transfers between devices, shifted(): return lax.ppermute(block, axis, route)  16.8 us
    another operation x3, other arithmetic  15.5 us
    all_to_all x1, waiting for transfers between devices, shards(): lax.all_to_all(mixer_terms, ('lat', 'lon'), split_axis=1, concat_axis=1,...  15 us
    all_to_all x1, waiting for transfers between devices, shards(): lax.all_to_all(filter_terms, 'lat', split_axis=1, concat_axis=1, tiled=True)  10.1 us
    unnamed x29, local copies, waits for them, and re-layouts  8.88 us
  transfers between devices with their start and end apart: 7, of which 5 were waited for; matrix products, arithmetic and copies ran while one was open for 9% of the time, Pallas kernels for 0%

profile of v1, /device:TPU:0, one launch (start us, length us, event | category | flops | bytes accessed | tf_op | source)
XLA Modules:
  0.0 311.3 jit_solution(17979140664822111312)
XLA Ops:
  0.6 0.0 copy-start
  0.6 1.7 copy-done
  2.3 5.0 %fusion.8 = (bf16[512,2304]{1,0:T(8,128)(2,1)}, f32[2304,512]{0,1:T(8,128)}) fusion(bf16[2304,512]{1,0:T(8,128)(2,1)S(1)} %bitcast.107, bf16[1,512,512]{2,1,0:T(8,128)(2,1)} %param.11), kind=kOutput, calls=%fused_computation.14 | convolution fusion | flops 1213857792 | bytes 9961472 | tf_op jit(solution)/shard_map/dot_general | solution.py:186
  7.3 6.2 %copy.62 = f32[2304,512]{1,0:T(8,128)} copy(f32[2304,512]{0,1:T(8,128)} %get-tuple-element.17) | data formatting | bytes 9437184 | tf_op jit(solution)/shard_map/dot_general | solution.py:186
  13.5 4.9 %fusion.9 = bf16[2304,512]{1,0:T(8,128)(2,1)S(1)} fusion(f32[2304,512]{1,0:T(8,128)} %copy.62, bf16[2304,512]{1,0:T(8,128)(2,1)} %bitcast.121, bf16[1,512,512]{2,1,0:T(8,128)(2,1)S(1)} %copy-done.11), kind=kOutput, calls=%fused_computation.15 | convolution fusion | flops 1219756032 | bytes 9961472 | tf_op jit(solution)/shard_map/dot_general | solution.py:189
  18.5 1.4 copy-done.12
  19.9 2.9 fusion.10
  22.8 2.8 broadcast_select_fusion.1
  25.7 0.4 collective-permute-start
  26.1 4.7 %multiply_convert_fusion = bf16[1,768,384]{1,2,0:T(8,128)(2,1)S(1)} fusion(f32[384]{0:T(512)S(1)} %get-tuple-element.18), kind=kLoop, calls=%fused_computation.46 | loop fusion | flops 3833856 | bytes 591360 | tf_op jit(solution)/shard_map/convert.7
  30.8 4.6 %multiply_convert_fusion.1 = bf16[1,768,384]{1,2,0:T(8,128)(2,1)S(1)} fusion(f32[384]{0:T(512)S(1)} %get-tuple-element.19), kind=kLoop, calls=%fused_computation.47 | loop fusion | flops 3244032 | bytes 591360 | tf_op jit(solution)/shard_map/convert.6
  35.5 0.1 fusion.27
  35.6 0.0 collective-permute-done
  35.6 3.3 %convert_bitcast_fusion = bf16[2,6,384,256]{3,2,1,0:T(8,128)(2,1)S(1)} fusion(bf16[6,384,256]{2,1,0:T(8,128)(2,1)} %collective-permute-done, bf16[6,384,256]{2,1,0:T(8,128)(2,1)S(1)} %get-tuple-element.10, bf16[2,384,384]{1,2,0:T(8,128)(2,1)S(1)} %get-tuple-element.13, bf16[2,384,384]{1,2,0:T(8,128)(2,1)S(1)} %get-tuple-element.12), kind=kOutput, calls=%fused_computation.23 | convolution fusion | flops 1820196864 | bytes 5898240 | tf_op jit(solution)/shard_map/tkc,rkm->rtmc/dot_general | solution.py:217
  38.9 3.9 %copy.66 = bf16[2,6,384,256]{3,0,1,2:T(2,128)(2,1)} copy(bf16[2,6,384,256]{3,2,1,0:T(8,128)(2,1)S(1)} %convert_bitcast_fusion) | data formatting | bytes 4718592 | tf_op jit(solution)/shard_map/convert_element_type | solution.py:222
  42.8 6.8 %all-to-all-start = ((bf16[2,6,384,256]{3,0,1,2:T(2,128)(2,1)}), bf16[2,6,384,256]{3,0,1,2:T(2,128)(2,1)}, u32[]{:S(2)}, u32[]{:S(2)}) async-start(bf16[2,6,384,256]{3,0,1,2:T(2,128)(2,1)} %copy.66), calls=%async_computation | async-start | bytes 4718592 | tf_op jit(solution)/shard_map/all_to_all | solution.py:223
  49.7 0.3 select_convert_fusion.swap_ref
  49.9 54.3 %all-to-all-done = bf16[2,6,384,256]{3,0,1,2:T(2,128)(2,1)} async-done(((bf16[2,6,384,256]{3,0,1,2:T(2,128)(2,1)}), bf16[2,6,384,256]{3,0,1,2:T(2,128)(2,1)}, u32[]{:S(2)}, u32[]{:S(2)}) %all-to-all-start) | async-done | bytes 2359328 | tf_op jit(solution)/shard_map/all_to_all | solution.py:223
  104.3 3.7 %copy.67 = bf16[2,6,8,48,256]{4,3,1,2,0:T(8,128)(2,1)} copy(bf16[2,6,8,48,256]{4,0,1,3,2:T(2,128)(2,1)} %bitcast.11) | data formatting | bytes 4718592 | tf_op jit(solution)/shard_map/all_to_all | solution.py:223
  108.0 65.9 %shard_map.102 = (f32[2,384,256]{2,1,0:T(8,128)S(1)}, bf16[2,48,48,256]{3,2,1,0:T(8,128)(2,1)S(1)}) custom-call(bf16[256,256]{1,0:T(8,128)(2,1)S(1)} %select_convert_fusion.swap_ref, bf16[2,48,48,256]{3,2,1,0:T(8,128)(2,1)} %bitcast.112, bf16[2,384,48,256]{3,2,1,0:T(8,128)(2,1)} %bitcast.111, f32[2,384,256]{2,1,0:T(8,128)S(1)} %bitcast.110, ...), custom_call_target="tpu_custom_call" | custom-call | flops 1811939328 | bytes 23592960 | tf_op jit(solution)/shard_map/pallas_call | solution.py:120
  173.9 1.8 copy.68
  175.7 4.4 %all-to-all-start.1 = ((bf16[2,48,48,256]{3,2,0,1:T(8,128)(2,1)}), bf16[2,48,48,256]{3,2,0,1:T(8,128)(2,1)}, u32[]{:S(2)}, u32[]{:S(2)}) async-start(bf16[2,48,48,256]{3,2,0,1:T(8,128)(2,1)} %copy.68), calls=%async_computation.1 | async-start | bytes 4718592 | tf_op jit(solution)/shard_map/all_to_all | solution.py:232
  180.1 6.2 %multiply_convert_fusion.2 = (bf16[1,768,384]{1,2,0:T(8,128)(2,1)}, bf16[1,768,384]{1,2,0:T(8,128)(2,1)}) fusion(), kind=kLoop, calls=%fused_computation.49 | loop fusion | flops 4128768 | bytes 1179648 | tf_op jit(solution)/shard_map/convert.8
  186.3 47.5 %all-to-all-done.1 = bf16[2,48,48,256]{3,2,0,1:T(8,128)(2,1)} async-done(((bf16[2,48,48,256]{3,2,0,1:T(8,128)(2,1)}), bf16[2,48,48,256]{3,2,0,1:T(8,128)(2,1)}, u32[]{:S(2)}, u32[]{:S(2)}) %all-to-all-start.1) | async-done | bytes 2359328 | tf_op jit(solution)/shard_map/all_to_all | solution.py:232
  233.8 2.0 copy.70
  235.8 1.4 copy-done.5
  237.2 2.2 fusion.15
  239.5 0.0 collective-permute-start.1
  239.5 1.4 convolution_convert_fusion.1
  240.9 0.2 copy-done.4
  241.1 0.7 copy-done.10
  241.8 1.4 fusion.16
  243.2 0.1 pad_maximum_fusion
  243.3 1.1 copy.77
  244.4 4.3 %all-to-all-start.3 = ((bf16[2,16,32,512]{3,2,0,1:T(8,128)(2,1)}), bf16[2,16,32,512]{3,2,0,1:T(8,128)(2,1)}, u32[]{:S(2)}, u32[]{:S(2)}) async-start(bf16[2,16,32,512]{3,2,0,1:T(8,128)(2,1)} %copy.77), calls=%async_computation.3 | async-start | bytes 2097152 | tf_op jit(solution)/shard_map/all_to_all | solution.py:226
  248.7 0.0 collective-permute-done.1
  248.7 3.4 %select_bitcast_fusion.1 = (bf16[1,6,384,256]{3,2,1,0:T(8,128)(2,1)S(1)}, bf16[1,6,384,256]{3,2,1,0:T(8,128)(2,1)S(1)}) fusion(bf16[6,384,256]{2,1,0:T(8,128)(2,1)} %collective-permute-done.1, pred[]{:T(512)S(6)} %eq.25, bf16[2,6,384,256]{3,2,1,0:T(8,128)(2,1)} %bitcast.117, s32[]{:T(128)S(6)} %select_n.87, bf16[1,768,384]{1,2,0:T(8,128)(2,1)} %get-tuple-element.26, ...), kind=kOutput, calls=%fused_computation.45 | convolution fusion | flops 908918784 | bytes 7077893 | tf_op jit(solution)/shard_map/rtmc,rkm->tkc/dot_general | solution.py:239
  252.2 2.1 fusion.4
  254.3 1.5 collective-permute-start.2
  255.8 0.8 copy.76
  256.6 15.0 %all-to-all-done.3 = bf16[2,16,32,512]{3,2,0,1:T(8,128)(2,1)} async-done(((bf16[2,16,32,512]{3,2,0,1:T(8,128)(2,1)}), bf16[2,16,32,512]{3,2,0,1:T(8,128)(2,1)}, u32[]{:S(2)}, u32[]{:S(2)}) %all-to-all-start.3) | async-done | bytes 1048608 | tf_op jit(solution)/shard_map/all_to_all | solution.py:226
  271.7 6.7 %all-to-all-start.2 = ((bf16[2,8,48,256]{3,2,0,1:T(8,128)(2,1)}), bf16[2,8,48,256]{3,2,0,1:T(8,128)(2,1)S(1)}, u32[]{:S(2)}, u32[]{:S(2)}) async-start(bf16[2,8,48,256]{3,2,0,1:T(8,128)(2,1)} %copy.76), calls=%async_computation.2 | async-start | bytes 786432 | tf_op jit(solution)/shard_map/all_to_all | solution.py:234
  278.4 1.4 convert_reduce_fusion
  279.8 0.7 fusion.46
  280.4 10.1 %all-to-all-done.2 = bf16[2,8,48,256]{3,2,0,1:T(8,128)(2,1)S(1)} async-done(((bf16[2,8,48,256]{3,2,0,1:T(8,128)(2,1)}), bf16[2,8,48,256]{3,2,0,1:T(8,128)(2,1)S(1)}, u32[]{:S(2)}, u32[]{:S(2)}) %all-to-all-start.2) | async-done | bytes 393248 | tf_op jit(solution)/shard_map/all_to_all | solution.py:234
  290.5 0.7 convert_reduce_fusion.1
  291.2 16.8 %collective-permute-done.2 = bf16[1,6,384,512]{3,2,1,0:T(8,128)(2,1)} collective-permute-done((bf16[1,6,384,512]{3,2,1,0:T(8,128)(2,1)}, bf16[1,6,384,512]{3,2,1,0:T(8,128)(2,1)}, u32[]{:S(2)}, u32[]{:S(2)}) %collective-permute-start.2) | collective-permute-done | bytes 2359328 | tf_op jit(solution)/shard_map/ppermute | solution.py:17
  308.0 3.4 %copy.90 = bf16[1,6,384,512]{3,2,1,0:T(8,128)(2,1)} copy(bf16[1,6,384,512]{3,2,1,0:T(8,128)(2,1)} %collective-permute-done.2) | data formatting | bytes 4718592
  (27 shorter events, 0.1 us)
Async XLA Ops:
  0.6 1.7 copy-start
  7.3 6.2 %copy-start.11 = (bf16[1,512,512]{2,1,0:T(8,128)(2,1)S(1)}, bf16[1,512,512]{2,1,0:T(8,128)(2,1)}, u32[]{:S(2)}) copy-start(bf16[1,512,512]{2,1,0:T(8,128)(2,1)} %param.12) | copy-start | bytes 1572868
  13.5 6.4 %copy-start.8 = (bf16[1,512,512]{2,1,0:T(8,128)(2,1)S(1)}, bf16[1,512,512]{2,1,0:T(8,128)(2,1)}, u32[]{:S(2)}) copy-start(bf16[1,512,512]{2,1,0:T(8,128)(2,1)} %param.11) | copy-start | bytes 1572868
  13.5 6.4 %copy-start.9 = (bf16[1,6,384,512]{3,2,1,0:T(8,128)(2,1)S(1)}, bf16[1,6,384,512]{3,2,1,0:T(8,128)(2,1)}, u32[]{:S(2)}) copy-start(bf16[1,6,384,512]{3,2,1,0:T(8,128)(2,1)} %param.8) | copy-start | bytes 7077892
  18.5 1.5 copy-start.12
  25.7 9.9 %collective-permute-start = (bf16[6,384,256]{2,1,0:T(8,128)(2,1)}, bf16[6,384,256]{2,1,0:T(8,128)(2,1)}, u32[]{:S(2)}, u32[]{:S(2)}) collective-permute-start(bf16[6,384,256]{2,1,0:T(8,128)(2,1)} %get-tuple-element.11), channel_id=1, source_target_pairs={{1,0},{0,1},{3,2},{2,3},{5,4},{4,5},{7,6},{6,7},{9,8},{8,9},{11,10... | collective-permute-start | bytes 3538952 | tf_op jit(solution)/shard_map/ppermute | solution.py:17
  42.8 61.5 %all-to-all-start = ((bf16[2,6,384,256]{3,0,1,2:T(2,128)(2,1)}), bf16[2,6,384,256]{3,0,1,2:T(2,128)(2,1)}, u32[]{:S(2)}, u32[]{:S(2)}) async-start(bf16[2,6,384,256]{3,0,1,2:T(2,128)(2,1)} %copy.66), calls=%async_computation | async-start | bytes 4718592 | tf_op jit(solution)/shard_map/all_to_all | solution.py:223
  104.3 3.7 %copy-start.1 = (bf16[48,384,48]{1,2,0:T(8,128)(2,1)S(1)}, bf16[48,384,48]{1,2,0:T(8,128)(2,1)}, u32[]{:S(2)}) copy-start(bf16[48,384,48]{1,2,0:T(8,128)(2,1)} %param.13) | copy-start | bytes 5308420
  104.3 3.7 %copy-start.2 = (f32[1,2,384,256]{3,2,1,0:T(8,128)S(1)}, f32[1,2,384,256]{3,2,1,0:T(8,128)}, u32[]{:S(2)}) copy-start(f32[1,2,384,256]{3,2,1,0:T(8,128)} %param.10) | copy-start | bytes 2359300
  175.7 58.1 %all-to-all-start.1 = ((bf16[2,48,48,256]{3,2,0,1:T(8,128)(2,1)}), bf16[2,48,48,256]{3,2,0,1:T(8,128)(2,1)}, u32[]{:S(2)}, u32[]{:S(2)}) async-start(bf16[2,48,48,256]{3,2,0,1:T(8,128)(2,1)} %copy.68), calls=%async_computation.1 | async-start | bytes 4718592 | tf_op jit(solution)/shard_map/all_to_all | solution.py:232
  233.8 3.4 %copy-start.6 = (bf16[1,768,384]{1,2,0:T(8,128)(2,1)S(1)}, bf16[1,768,384]{1,2,0:T(8,128)(2,1)}, u32[]{:S(2)}) copy-start(bf16[1,768,384]{1,2,0:T(8,128)(2,1)} %get-tuple-element.26) | copy-start | bytes 1769476
  233.8 3.4 %copy-start.7 = (bf16[1,768,384]{1,2,0:T(8,128)(2,1)S(1)}, bf16[1,768,384]{1,2,0:T(8,128)(2,1)}, u32[]{:S(2)}) copy-start(bf16[1,768,384]{1,2,0:T(8,128)(2,1)} %get-tuple-element.27) | copy-start | bytes 1769476
  235.8 1.5 copy-start.5
  237.2 2.2 copy-start.13
  239.5 1.7 copy-start.4
  239.5 2.4 copy-start.10
  239.5 9.3 %collective-permute-start.1 = (bf16[6,384,256]{2,1,0:T(8,128)(2,1)}, bf16[6,384,256]{2,1,0:T(8,128)(2,1)}, u32[]{:S(2)}, u32[]{:S(2)}) collective-permute-start(bf16[6,384,256]{2,1,0:T(8,128)(2,1)} %fusion.15), channel_id=1, source_target_pairs={{1,0},{0,1},{3,2},{2,3},{5,4},{4,5},{7,6},{6,7},{9,8},{8,9},{11,10... | collective-permute-start | bytes 3538952 | tf_op jit(solution)/shard_map/ppermute | solution.py:17
  244.4 27.3 %all-to-all-start.3 = ((bf16[2,16,32,512]{3,2,0,1:T(8,128)(2,1)}), bf16[2,16,32,512]{3,2,0,1:T(8,128)(2,1)}, u32[]{:S(2)}, u32[]{:S(2)}) async-start(bf16[2,16,32,512]{3,2,0,1:T(8,128)(2,1)} %copy.77), calls=%async_computation.3 | async-start | bytes 2097152 | tf_op jit(solution)/shard_map/all_to_all | solution.py:226
  248.7 3.5 %copy-start.3 = (bf16[2304,512]{1,0:T(8,128)(2,1)S(1)}, bf16[2304,512]{1,0:T(8,128)(2,1)}, u32[]{:S(2)}) copy-start(bf16[2304,512]{1,0:T(8,128)(2,1)} %fusion.10) | copy-start | bytes 7077892
  254.3 53.7 %collective-permute-start.2 = (bf16[1,6,384,512]{3,2,1,0:T(8,128)(2,1)}, bf16[1,6,384,512]{3,2,1,0:T(8,128)(2,1)}, u32[]{:S(2)}, u32[]{:S(2)}) collective-permute-start(bf16[1,6,384,512]{3,2,1,0:T(8,128)(2,1)} %fusion.4), channel_id=1, source_target_pairs={{16,0},{0,16},{17,1},{1,17},{18,2},{2,18},{19,3},{3,19},{20,4},{4,... | collective-permute-start | bytes 7077896 | tf_op jit(solution)/shard_map/ppermute | solution.py:17
  271.7 18.9 %all-to-all-start.2 = ((bf16[2,8,48,256]{3,2,0,1:T(8,128)(2,1)}), bf16[2,8,48,256]{3,2,0,1:T(8,128)(2,1)S(1)}, u32[]{:S(2)}, u32[]{:S(2)}) async-start(bf16[2,8,48,256]{3,2,0,1:T(8,128)(2,1)} %copy.76), calls=%async_computation.2 | async-start | bytes 786432 | tf_op jit(solution)/shard_map/all_to_all | solution.py:234

commit v2 on v1

v2 whole, which is shorter than its diff:
```python
import math

import jax
import jax.numpy as jnp
import numpy as np
from jax import lax
from jax.experimental import pallas as pl
from jax.experimental.pallas import tpu as pltpu
from jax.sharding import PartitionSpec as P

MODES = 384


def shifted(block, axis, distance):
    devices = range(lax.axis_size(axis))
    route = [((i - distance) % len(devices), i) for i in devices]
    return lax.ppermute(block, axis, route)


def transform_tables(period, orders_kept):
    positions = np.arange(period, dtype=np.int32)
    orders = np.arange(orders_kept, dtype=np.int32)
    phases = positions[:, None] * orders[None, :] % period
    angles = phases.astype(np.float32) * np.float32(2.0 * math.pi / period)
    factor = np.float32(1.0 / math.sqrt(period))
    cosine = np.cos(angles) * factor
    sine_part = np.sin(angles) * factor
    doubled = np.where(orders == 0, 1.0, 2.0).astype(np.float32)[None, :]
    synthesis = np.stack([cosine * doubled, -sine_part * doubled]).astype(jnp.bfloat16)
    analysis = np.stack([cosine, -sine_part]).astype(jnp.bfloat16)
    return (synthesis, analysis)


def gelu_pair(pre_active):
    normal_cdf = 0.5 * (1.0 + lax.erf(pre_active * (1.0 / math.sqrt(2.0))))
    density = jnp.exp(-0.5 * pre_active * pre_active) * (1.0 / math.sqrt(2.0 * math.pi))
    return (pre_active * normal_cdf, normal_cdf + pre_active * density)

GROUP = 16


def swap_matrix():
    row = lax.broadcasted_iota(jnp.int32, (GROUP * GROUP, GROUP * GROUP), 0)
    column = lax.broadcasted_iota(jnp.int32, (GROUP * GROUP, GROUP * GROUP), 1)
    partner = row % GROUP * GROUP + row // GROUP
    return jnp.where(partner == column, 1.0, 0.0).astype(jnp.bfloat16)


def swapped(matrix, block):
    flat = block.reshape(GROUP * GROUP, block.shape[2])
    turned = jnp.dot(matrix, flat, preferred_element_type=jnp.float32)
    return turned.astype(jnp.bfloat16).reshape(block.shape)


def middle_kernel(
    swap_ref, x_ref, s_ref, w_ref, map_ref, filter_ref, out_ref, x_major, s_major, out_major
):
    owners, _, lats, _, width = x_ref.shape
    bands_count = owners * lats
    degrees = s_ref.shape[1]
    step = pl.program_id(0)
    matrix = swap_ref[...]

    @pl.when(step == 0)
    def _():
        out_major[...] = jnp.zeros_like(out_major)
        for part in range(2):
            lanes = slice(part * width, (part + 1) * width)
            x_all = x_ref[:, part].reshape(bands_count, GROUP, width)
            for piece in range(bands_count // GROUP):
                rows = slice(piece * GROUP, (piece + 1) * GROUP)
                x_major[:, rows, lanes] = swapped(matrix, x_all[rows])

    for part in range(2):
        lanes = slice(part * width, (part + 1) * width)
        for piece in range(degrees // GROUP):
            rows = slice(piece * GROUP, (piece + 1) * GROUP)
            s_major[:, rows, lanes] = swapped(matrix, s_ref[part, rows])

    filter_ref[...] = jnp.zeros_like(filter_ref)

    @pl.loop(0, GROUP)
    def _(order):
        maps = map_ref[order]
        degree = lax.dot_general(
            maps, x_major[order], (((0,), (0,)), ((), ())), preferred_element_type=jnp.float32
        )
        real, imag = degree[:, :width], degree[:, width:]
        saved_real = s_major[order, :, :width].astype(jnp.float32)
        saved_imag = s_major[order, :, width:].astype(jnp.float32)
        filter_ref[0] += real * saved_real + imag * saved_imag
        filter_ref[1] += imag * saved_real - real * saved_imag
        weight_real, weight_imag = w_ref[0], w_ref[1]
        coef_real = (weight_real * real + weight_imag * imag).astype(jnp.bfloat16)
        coef_imag = (weight_real * imag - weight_imag * real).astype(jnp.bfloat16)
        out_major[order, :, :width] += jnp.dot(
            maps, coef_real, preferred_element_type=jnp.float32
        )
        out_major[order, :, width:] += jnp.dot(
            maps, coef_imag, preferred_element_type=jnp.float32
        )

    @pl.when(step == pl.num_programs(0) - 1)
    def _():
        for part in range(2):
            lanes = slice(part * width, (part + 1) * width)
            pieces = []
            for piece in range(bands_count // GROUP):
                rows = slice(piece * GROUP, (piece + 1) * GROUP)
                block = out_major[:, rows, lanes].astype(jnp.bfloat16)
                pieces.append(swapped(matrix, block))
            whole = jnp.concatenate(pieces, axis=0)
            out_ref[:, part] = whole.reshape(owners, lats, GROUP, width)


BLOCK = 384


def middle(group, bands, saved, weights, maps):
    owners, _, lats, _, width = bands.shape
    degrees = saved.shape[1]
    steps = degrees // BLOCK
    return pl.pallas_call(
        middle_kernel,
        grid=(steps,),
        in_specs=[
            pl.BlockSpec((GROUP * GROUP, GROUP * GROUP), lambda i: (0, 0)),
            pl.BlockSpec(bands.shape, lambda i: (0, 0, 0, 0, 0)),
            pl.BlockSpec((2, BLOCK, GROUP, width), lambda i: (0, i, group, 0)),
            pl.BlockSpec((2, BLOCK, width), lambda i: (0, i, 0)),
            pl.BlockSpec((GROUP, owners * lats, BLOCK), lambda i: (group, 0, i)),
        ],
        out_specs=[
            pl.BlockSpec((2, BLOCK, width), lambda i: (0, i, 0)),
            pl.BlockSpec(bands.shape, lambda i: (0, 0, 0, 0, 0)),
        ],
        out_shape=[
            jax.ShapeDtypeStruct((2, degrees, width), jnp.float32),
            jax.ShapeDtypeStruct(bands.shape, jnp.bfloat16),
        ],
        scratch_shapes=[
            pltpu.VMEM((GROUP, owners * lats, 2 * width), jnp.bfloat16),
            pltpu.VMEM((GROUP, BLOCK, 2 * width), jnp.bfloat16),
            pltpu.VMEM((GROUP, owners * lats, 2 * width), jnp.float32),
        ],
        compiler_params=pltpu.CompilerParams(vmem_limit_bytes=40 << 20),
        cost_estimate=pl.CostEstimate(
            flops=20_000_000_000, bytes_accessed=saved.size * 2 // 3, transcendentals=0
        ),
    )(swap_matrix(), bands, saved, weights, jnp.swapaxes(maps, 1, 2))


def middle_plain(group, bands, saved, weights, maps):
    owners, _, lats, orders, width = bands.shape
    order_major = jnp.swapaxes(bands, 0, 1).reshape(2, owners * lats, orders, width)
    degree_grad = jnp.einsum(
        "mlt,rtmc->rlmc", maps, order_major, preferred_element_type=jnp.float32
    )
    saved = saved.astype(jnp.float32)
    filter_terms = jnp.stack(
        [
            jnp.sum(degree_grad[0] * saved[0] + degree_grad[1] * saved[1], axis=1),
            jnp.sum(degree_grad[1] * saved[0] - degree_grad[0] * saved[1], axis=1),
        ]
    )
    real, imag = weights[0][:, None, :], weights[1][:, None, :]
    coef_grad = jnp.stack(
        [
            real * degree_grad[0] + imag * degree_grad[1],
            real * degree_grad[1] - imag * degree_grad[0],
        ]
    ).astype(jnp.bfloat16)
    band_grad = jnp.einsum(
        "mlt,rlmc->rtmc", maps, coef_grad, preferred_element_type=jnp.float32
    ).astype(jnp.bfloat16)
    band_grad = jnp.swapaxes(band_grad.reshape(2, owners, lats, orders, width), 0, 1)
    return filter_terms, band_grad


def mixer_kernel(
    hidden_ref, grad_ref, up_ref, down_ref, rows_ref, low_ref, high_ref, terms_ref, up_sum, down_sum
):
    step = pl.program_id(0)
    hidden, grad = hidden_ref[0], grad_ref[0]
    pre_active = jnp.dot(hidden, up_ref[...], preferred_element_type=jnp.float32)
    activation, slopes = gelu_pair(pre_active)
    carried = lax.dot_general(
        grad, down_ref[...], (((1,), (1,)), ((), ())), preferred_element_type=jnp.float32
    )
    grad_pre = (carried * slopes).astype(jnp.bfloat16)
    back_rows = lax.dot_general(
        grad_pre, up_ref[...], (((1,), (1,)), ((), ())), preferred_element_type=jnp.float32
    )
    grad_hidden = (grad.astype(jnp.float32) + back_rows).astype(jnp.bfloat16)
    rows_ref[0] = grad_hidden
    half = grad_hidden.shape[1] // 2
    low_ref[0] = grad_hidden[:, :half]
    high_ref[0] = grad_hidden[:, half:]

    @pl.when(step == 0)
    def _():
        up_sum[...] = jnp.zeros_like(up_sum)
        down_sum[...] = jnp.zeros_like(down_sum)

    across = (((0,), (0,)), ((), ()))
    up_sum[...] += lax.dot_general(hidden, grad_pre, across, preferred_element_type=jnp.float32)
    down_sum[...] += lax.dot_general(
        activation.astype(jnp.bfloat16), grad, across, preferred_element_type=jnp.float32
    )

    @pl.when(step == pl.num_programs(0) - 1)
    def _():
        terms_ref[0] = up_sum[...].astype(jnp.bfloat16)
        terms_ref[1] = down_sum[...].astype(jnp.bfloat16)


def mixer(hidden, grad, up_matrix, down_matrix):
    lats, longitudes, embed = hidden.shape
    units = up_matrix.shape[1]
    rows = pl.BlockSpec((1, longitudes, embed), lambda i: (i, 0, 0))
    halves = pl.BlockSpec((1, longitudes, embed // 2), lambda i: (i, 0, 0))
    return pl.pallas_call(
        mixer_kernel,
        grid=(lats,),
        in_specs=[
            rows,
            rows,
            pl.BlockSpec(up_matrix.shape, lambda i: (0, 0)),
            pl.BlockSpec(down_matrix.shape, lambda i: (0, 0)),
        ],
        out_specs=[rows, halves, halves, pl.BlockSpec((2, embed, units), lambda i: (0, 0, 0))],
        out_shape=[
            jax.ShapeDtypeStruct(hidden.shape, jnp.bfloat16),
            jax.ShapeDtypeStruct((lats, longitudes, embed // 2), jnp.bfloat16),
            jax.ShapeDtypeStruct((lats, longitudes, embed // 2), jnp.bfloat16),
            jax.ShapeDtypeStruct((2, embed, units), jnp.bfloat16),
        ],
        scratch_shapes=[
            pltpu.VMEM((embed, units), jnp.float32),
            pltpu.VMEM((units, embed), jnp.float32),
        ],
        compiler_params=pltpu.CompilerParams(vmem_limit_bytes=40 << 20),
    )(hidden, grad, up_matrix, down_matrix)


def back_kernel(table_ref, *refs):
    *bands, near_ref, far_ref = refs
    owners, _, _, orders, width = bands[0].shape
    stacked = jnp.concatenate(
        [ref[:, :, 0].reshape(owners * 2 * orders, width) for ref in bands], axis=0
    )
    length = near_ref.shape[1]
    far_ref[0] = jnp.dot(
        table_ref[length:], stacked, preferred_element_type=jnp.float32
    ).astype(jnp.bfloat16)
    near_ref[0] = jnp.dot(
        table_ref[:length], stacked, preferred_element_type=jnp.float32
    ).astype(jnp.bfloat16)


def back(table, bands):
    owners, _, lats, orders, width = bands[0].shape
    period = table.shape[0]
    out = pl.BlockSpec((1, period // 2, width), lambda i: (i, 0, 0))
    shape = jax.ShapeDtypeStruct((lats, period // 2, width), jnp.bfloat16)
    block = pl.BlockSpec((owners, 2, 1, orders, width), lambda i: (0, 0, i, 0, 0))
    return pl.pallas_call(
        back_kernel,
        grid=(lats,),
        in_specs=[pl.BlockSpec(table.shape, lambda i: (0, 0))] + [block] * len(bands),
        out_specs=[out, out],
        out_shape=[shape, shape],
        compiler_params=pltpu.CompilerParams(vmem_limit_bytes=40 << 20),
    )(table, *bands)


def back_plain(table, bands):
    stacked = jnp.concatenate(
        [jnp.transpose(x, (2, 0, 1, 3, 4)).reshape(x.shape[2], -1, x.shape[4]) for x in bands],
        axis=1,
    )
    whole = jnp.einsum("kq,tqc->tkc", table, stacked, preferred_element_type=jnp.float32)
    whole = whole.astype(jnp.bfloat16)
    length = table.shape[0] // 2
    return whole[:, :length], whole[:, length:]


def shards(
    block_hidden, incoming_grad, saved_coeffs, filter_weights, up_weight, down_weight, latitude_maps
):
    band_rows = block_hidden.shape[1]
    slab_width = block_hidden.shape[2]
    embed = block_hidden.shape[3]
    grad_grid, low, high, mixer_terms = mixer(
        block_hidden[0], incoming_grad[0], up_weight[0], down_weight[0]
    )
    group_count = lax.axis_size(("lat", "lon"))
    lat_count = lax.axis_size("lat")
    lon_index = lax.axis_index("lon")
    half = embed // 2
    period = slab_width * 2
    local_orders = latitude_maps.shape[0]
    fits = local_orders % GROUP == 0 and band_rows * lat_count <= 64
    width = GROUP if fits else local_orders
    groups = local_orders // width
    synthesis, analysis = transform_tables(period, MODES)

    def rolled(table):
        table = jnp.asarray(np.concatenate([table, table[:slab_width]], axis=0))
        return lax.dynamic_slice_in_dim(table, lon_index * slab_width, period, 0)

    def by_group(table):
        return table.reshape(2, period, lat_count, groups, width).transpose(1, 3, 2, 0, 4)

    other = jnp.where(lon_index == 0, high, low)
    own = jnp.where(lon_index == 0, low, high)
    theirs = shifted(other, "lon", 1)
    handed_rows = shifted(grad_grid, "section", 1)
    all_rows = jnp.concatenate([own, theirs], axis=1)
    synthesis = rolled(by_group(synthesis))
    analysis = rolled(by_group(analysis).reshape(period, -1))
    bands, filter_terms = [], 0.0
    for group in range(groups):
        spectrum = jnp.einsum(
            "tkc,kdrj->drtjc", all_rows, synthesis[:, group], preferred_element_type=jnp.float32
        ).astype(jnp.bfloat16)
        bands.append(lax.all_to_all(spectrum, "lat", split_axis=0, concat_axis=0, tiled=True))
    returned = []
    flipped = []
    for group in range(groups):
        if group == 1:
            bands[1], last_bands = lax.optimization_barrier((bands[1], back_bands))
            back_bands = last_bands
        if group >= 1:
            flipped.append(shifted(back_bands, "section", 1))
        if group == 2:
            bands[2], flipped[0], handed_rows = lax.optimization_barrier(
                (bands[2], flipped[0], handed_rows)
            )
        if group >= 2:
            returned.append(
                lax.all_to_all(flipped[group - 2], "lat", split_axis=0, concat_axis=0, tiled=True)
            )
        terms, back_bands = (middle if fits else middle_plain)(
            group, bands[group], saved_coeffs[0], filter_weights[0], latitude_maps
        )
        filter_terms = filter_terms + terms
    if returned:
        back_bands, returned[-1] = lax.optimization_barrier((back_bands, returned[-1]))
    flipped.append(shifted(back_bands, "section", 1))
    for block in flipped[len(returned) :]:
        returned.append(lax.all_to_all(block, "lat", split_axis=0, concat_axis=0, tiled=True))
    filter_terms = filter_terms.reshape(2, lat_count, -1, half).astype(jnp.bfloat16)
    mixer_terms, filter_terms, returned[-1] = lax.optimization_barrier(
        (mixer_terms, filter_terms, returned[-1])
    )
    filter_parts = lax.all_to_all(filter_terms, "lat", split_axis=1, concat_axis=1, tiled=True)
    filter_grad = jnp.sum(filter_parts.astype(jnp.float32), axis=1)
    mixer_terms = mixer_terms.reshape(2, group_count, -1, mixer_terms.shape[2])
    mixer_parts = lax.all_to_all(mixer_terms, ("lat", "lon"), split_axis=1, concat_axis=1, tiled=True)
    up_grad, down_grad = jnp.sum(mixer_parts.astype(jnp.float32), axis=1)
    own_back, for_other = (back if fits else back_plain)(analysis, returned)
    their_back = shifted(for_other, "lon", 1)
    grid_back = jnp.concatenate(
        [
            jnp.where(lon_index == 0, own_back, their_back),
            jnp.where(lon_index == 0, their_back, own_back),
        ],
        axis=2,
    )
    passed = handed_rows.astype(jnp.float32) + grid_back.astype(jnp.float32)
    handed_grad = passed.astype(jnp.bfloat16)[None]
    return (handed_grad, filter_grad[None], up_grad[None], down_grad[None])


def solution(mesh):
    in_specs = (
        P("section", "lat", "lon", None),
        P("section", "lat", "lon", None),
        P("section", None, None, "lat", "lon"),
        P("section", None, None, "lon"),
        P("section", None, None),
        P("section", None, None),
        P("lat", None, None),
    )
    out_specs = (
        P("section", "lat", "lon", None),
        P("section", None, "lat", "lon"),
        P("section", ("lat", "lon"), None),
        P("section", ("lat", "lon"), None),
    )
    return jax.shard_map(shards, mesh=mesh, in_specs=in_specs, out_specs=out_specs, check_vma=False)
```

time: 312 us -> 273 us (0.88)
  starting transfers between devices: 24.2 us -> 46.3 us
  waiting for transfers between devices: 144 us -> 126 us
  other arithmetic: 23.1 us -> 7.88 us
  matrix products: 24.6 us -> 10 us
  Pallas kernels: 65.9 us -> 56.3 us
  local copies, waits for them, and re-layouts: 28.9 us -> 22.7 us
    all_to_all x2 -> x6, waiting for transfers between devices: 102 us -> 46.1 us  [the longest x3 32.1 us: shards(): lax.all_to_all(spectrum, 'lat', split_axis=0, concat_axis=0, tiled=True)]
    ppermute x3 -> x6, waiting for transfers between devices: 16.8 us -> 60.3 us  [shifted(): return lax.ppermute(block, axis, route)]
    all_to_all x2 -> x6, starting transfers between devices: 11.2 us -> 31.5 us  [the longest x3 14.3 us: shards(): lax.all_to_all(spectrum, 'lat', split_axis=0, concat_axis=0, tiled=True)]
    another operation x5 -> x0, other arithmetic: 15.7 us -> none
    dot_general x8 -> x3, matrix products: 24.6 us -> 10 us  [shards(): jnp.einsum('tkc,kdrj->drtjc', all_rows, synthesis[:, group], preferred_el...]
    unnamed x29 -> x34, local copies, waits for them, and re-layouts: 8.88 us -> 18.9 us
    pallas_call x1 -> x5, Pallas kernels: 65.9 us -> 56.3 us  [the longest x3 42.9 us: middle(): pl.pallas_call(middle_kernel, grid=(steps,), in_specs=[pl.BlockSpec((GROU...]
    dot_general x1 -> x0, local copies, waits for them, and re-layouts: 6.19 us -> none  [shards(): jnp.dot(token_rows, up_matrix, preferred_element_type=jnp.float32)]
  transfers between devices with their start and end apart: 7 -> 14, of which waited for: 5 -> 12; matrix products, arithmetic and copies ran while one was open for 9% -> 7% of each run, Pallas kernels for 0% -> 17%
where the time goes in v2:
time: 273 us; the launch traced here: 270 us
  waiting for transfers between devices  126 us (46%)
  Pallas kernels  56.3 us (21%)
  starting transfers between devices  46.3 us (17%)
  local copies, waits for them, and re-layouts  22.7 us (8%)
  matrix products  10 us (4%)
  other arithmetic  7.88 us (3%)
    ppermute x6, waiting for transfers between devices, shifted(): return lax.ppermute(block, axis, route)  60.3 us
    pallas_call x3, Pallas kernels, middle(): pl.pallas_call(middle_kernel, grid=(steps,), in_specs=[pl.BlockSpec((GROU...  42.9 us
    all_to_all x3, waiting for transfers between devices, shards(): lax.all_to_all(spectrum, 'lat', split_axis=0, concat_axis=0, tiled=True)  32.1 us
    unnamed x34, local copies, waits for them, and re-layouts  18.9 us
    all_to_all x3, starting transfers between devices, shards(): lax.all_to_all(spectrum, 'lat', split_axis=0, concat_axis=0, tiled=True)  14.3 us
    all_to_all x2, waiting for transfers between devices, shards(): lax.all_to_all(block, 'lat', split_axis=0, concat_axis=0, tiled=True)  13.5 us
    all_to_all x1, waiting for transfers between devices, shards(): lax.all_to_all(mixer_terms, ('lat', 'lon'), split_axis=1, concat_axis=1,...  11.7 us
    all_to_all x2, starting transfers between devices, shards(): lax.all_to_all(block, 'lat', split_axis=0, concat_axis=0, tiled=True)  11.4 us
  transfers between devices with their start and end apart: 14, of which 12 were waited for; matrix products, arithmetic and copies ran while one was open for 7% of the time, Pallas kernels for 17%

profile of v2, /device:TPU:0, one launch (start us, length us, event | category | flops | bytes accessed | tf_op | source)
XLA Modules:
  0.0 270.3 jit_solution(14026549866539127289)
XLA Ops:
  0.6 1.7 copy-done
  2.3 1.7 copy-done.1
  4.0 1.0 copy-done.5
  5.0 1.0 copy-done.6
  6.1 10.3 %shard_map.120 = (bf16[6,384,512]{2,1,0:T(8,128)(2,1)S(1)}, bf16[6,384,256]{2,1,0:T(8,128)(2,1)S(1)}, bf16[6,384,256]{2,1,0:T(8,128)(2,1)S(1)}, bf16[2,512,512]{2,1,0:T(8,128)(2,1)S(1)}) custom-call(bf16[6,384,512]{2,1,0:T(8,128)(2,1)S(1)} %bitcast.43, bf16[6,384,512]{2,1,0:T(8,128)(2,1)S(1)} %bitcast.44, bf16[512,512]{1,0:T(8,128)(2,1)S(1)} %bitcast.46, ...), custom_call_target="tpu_custom_call" | custom-call | tf_op jit(solution)/shard_map/pallas_call | solution.py:222
  16.6 1.2 copy-done.7
  18.3 2.6 collective-permute-done
  20.9 3.1 %fusion.3 = bf16[8,2,6,16,256]{4,3,2,1,0:T(8,128)(2,1)} fusion(bf16[6,384,256]{2,1,0:T(8,128)(2,1)} %collective-permute-done, bf16[6,384,256]{2,1,0:T(8,128)(2,1)S(1)} %get-tuple-element.50, bf16[1152,3,8,2,16]{0,4,3,2,1:T(8,128)(2,1)} %constant.59.clone, s32[]{:T(128)S(6)} %select_n.60), kind=kOutput, calls=%fused_computation.9 | convolution fusion | flops 609091584 | bytes 3538948 | tf_op jit(solution)/shard_map/tkc,kdrj->drtjc/dot_general | solution.py:324
  24.0 7.2 %all-to-all-start.2 = ((bf16[8,2,6,16,256]{4,3,2,1,0:T(8,128)(2,1)}), bf16[8,2,6,16,256]{4,3,2,1,0:T(8,128)(2,1)S(1)}, u32[]{:S(2)}, u32[]{:S(2)}) async-start(bf16[8,2,6,16,256]{4,3,2,1,0:T(8,128)(2,1)} %fusion.3), calls=%async_computation.2 | async-start | bytes 1572864 | tf_op jit(solution)/shard_map/all_to_all | solution.py:327
  31.2 3.4 %fusion.2 = bf16[8,2,6,16,256]{4,3,2,1,0:T(8,128)(2,1)} fusion(bf16[6,384,256]{2,1,0:T(8,128)(2,1)} %collective-permute-done, bf16[6,384,256]{2,1,0:T(8,128)(2,1)} %copy-done.15, bf16[1152,3,8,2,16]{0,4,3,2,1:T(8,128)(2,1)} %constant.59.clone, s32[]{:T(128)S(6)} %select_n.60, s32[]{:T(128)S(6)} %add.46), kind=kOutput, calls=%fused_computation.8 | convolution fusion | flops 609091584 | bytes 3538952 | tf_op jit(solution)/shard_map/tkc,kdrj->drtjc/dot_general | solution.py:324
  34.6 17.0 %all-to-all-done.2.x_ref = bf16[8,2,6,16,256]{4,3,2,1,0:T(8,128)(2,1)S(1)} async-done(((bf16[8,2,6,16,256]{4,3,2,1,0:T(8,128)(2,1)}), bf16[8,2,6,16,256]{4,3,2,1,0:T(8,128)(2,1)S(1)}, u32[]{:S(2)}, u32[]{:S(2)}) %all-to-all-start.2) | async-done | bytes 786464 | tf_op jit(solution)/shard_map/all_to_all | solution.py:327
  51.6 3.6 %all-to-all-start.1 = ((bf16[8,2,6,16,256]{4,3,2,1,0:T(8,128)(2,1)}), bf16[8,2,6,16,256]{4,3,2,1,0:T(8,128)(2,1)S(1)}, u32[]{:S(2)}, u32[]{:S(2)}) async-start(bf16[8,2,6,16,256]{4,3,2,1,0:T(8,128)(2,1)} %fusion.2), calls=%async_computation.1 | async-start | bytes 1572864 | tf_op jit(solution)/shard_map/all_to_all | solution.py:327
  55.2 1.5 collective-permute-start.2
  57.1 3.5 %fusion.1 = bf16[8,2,6,16,256]{4,3,2,1,0:T(8,128)(2,1)} fusion(bf16[6,384,256]{2,1,0:T(8,128)(2,1)} %collective-permute-done, bf16[6,384,256]{2,1,0:T(8,128)(2,1)} %copy-done.15, bf16[1152,3,8,2,16]{0,4,3,2,1:T(8,128)(2,1)} %constant.59.clone, s32[]{:T(128)S(6)} %select_n.60, s32[]{:T(128)S(6)} %add.45), kind=kOutput, calls=%fused_computation.7 | convolution fusion | flops 609091584 | bytes 3538952 | tf_op jit(solution)/shard_map/tkc,kdrj->drtjc/dot_general | solution.py:324
  60.6 15.1 %all-to-all-done.1.x_ref = bf16[8,2,6,16,256]{4,3,2,1,0:T(8,128)(2,1)S(1)} async-done(((bf16[8,2,6,16,256]{4,3,2,1,0:T(8,128)(2,1)}), bf16[8,2,6,16,256]{4,3,2,1,0:T(8,128)(2,1)S(1)}, u32[]{:S(2)}, u32[]{:S(2)}) %all-to-all-start.1) | async-done | bytes 786464 | tf_op jit(solution)/shard_map/all_to_all | solution.py:327
  75.6 3.5 %all-to-all-start = ((bf16[8,2,6,16,256]{4,3,2,1,0:T(8,128)(2,1)}), bf16[8,2,6,16,256]{4,3,2,1,0:T(8,128)(2,1)S(1)}, u32[]{:S(2)}, u32[]{:S(2)}) async-start(bf16[8,2,6,16,256]{4,3,2,1,0:T(8,128)(2,1)} %fusion.1), calls=%async_computation | async-start | bytes 1572864 | tf_op jit(solution)/shard_map/all_to_all | solution.py:327
  79.2 1.5 copy-done.8
  80.7 1.1 copy-done.11
  81.8 14.9 %shard_map.121 = (f32[2,384,256]{2,1,0:T(8,128)S(1)}, bf16[8,2,6,16,256]{4,3,2,1,0:T(8,128)(2,1)}) custom-call(bf16[256,256]{1,0:T(8,128)(2,1)S(1)} %select_convert_fusion.swap_ref, bf16[8,2,6,16,256]{4,3,2,1,0:T(8,128)(2,1)S(1)} %all-to-all-done.2.x_ref, bf16[2,384,48,256]{3,2,1,0:T(8,128)(2,1)} %bitcast.56, f32[2,384,256]{2,1,0:T(8,128)S(1)} %bitcast.51, ...), custom_call_target="tpu_custom_call" | custom-call | flops 20000000000 | bytes 6291456 | tf_op jit(solution)/shard_map/pallas_call | solution.py:123
  96.7 0.9 copy-done.2
  97.6 1.5 collective-permute-start.1
  99.1 10.7 %collective-permute-done.2 = bf16[6,384,512]{2,1,0:T(8,128)(2,1)} collective-permute-done((bf16[6,384,512]{2,1,0:T(8,128)(2,1)}, bf16[6,384,512]{2,1,0:T(8,128)(2,1)}, u32[]{:S(2)}, u32[]{:S(2)}) %collective-permute-start.2) | collective-permute-done | bytes 2359328 | tf_op jit(solution)/shard_map/ppermute | solution.py:17
  109.8 15.5 %collective-permute-done.1 = bf16[8,2,6,16,256]{4,3,2,1,0:T(8,128)(2,1)} collective-permute-done((bf16[8,2,6,16,256]{4,3,2,1,0:T(8,128)(2,1)}, bf16[8,2,6,16,256]{4,3,2,1,0:T(8,128)(2,1)}, u32[]{:S(2)}, u32[]{:S(2)}) %collective-permute-start.1) | collective-permute-done | bytes 786464 | tf_op jit(solution)/shard_map/ppermute | solution.py:17
  125.3 5.7 %all-to-all-start.3 = ((bf16[8,2,6,16,256]{4,3,2,1,0:T(8,128)(2,1)}), bf16[8,2,6,16,256]{4,3,2,1,0:T(8,128)(2,1)S(1)}, u32[]{:S(2)}, u32[]{:S(2)}) async-start(bf16[8,2,6,16,256]{4,3,2,1,0:T(8,128)(2,1)} %collective-permute-done.1), calls=%async_computation.3 | async-start | bytes 1572864 | tf_op jit(solution)/shard_map/all_to_all | solution.py:342
  131.0 1.5 copy-done.9
  132.5 1.1 copy-done.12
  133.6 14.0 %shard_map.122 = (f32[2,384,256]{2,1,0:T(8,128)S(1)}, bf16[8,2,6,16,256]{4,3,2,1,0:T(8,128)(2,1)S(1)}) custom-call(bf16[256,256]{1,0:T(8,128)(2,1)S(1)} %select_convert_fusion.swap_ref, bf16[8,2,6,16,256]{4,3,2,1,0:T(8,128)(2,1)S(1)} %all-to-all-done.x_ref, bf16[2,384,48,256]{3,2,1,0:T(8,128)(2,1)} %bitcast.57, f32[2,384,256]{2,1,0:T(8,128)S(1)} %bitcast.52, ...), custom_call_target="tpu_custom_call" | custom-call | flops 20000000000 | bytes 6291456 | tf_op jit(solution)/shard_map/pallas_call | solution.py:123
  150.0 1.5 collective-permute-start.4
  151.5 16.0 %collective-permute-done.4 = bf16[8,2,6,16,256]{4,3,2,1,0:T(8,128)(2,1)} collective-permute-done((bf16[8,2,6,16,256]{4,3,2,1,0:T(8,128)(2,1)}, bf16[8,2,6,16,256]{4,3,2,1,0:T(8,128)(2,1)}, u32[]{:S(2)}, u32[]{:S(2)}) %collective-permute-start.4) | collective-permute-done | bytes 786464 | tf_op jit(solution)/shard_map/ppermute | solution.py:17
  167.4 5.7 %all-to-all-start.5 = ((bf16[8,2,6,16,256]{4,3,2,1,0:T(8,128)(2,1)}), bf16[8,2,6,16,256]{4,3,2,1,0:T(8,128)(2,1)S(1)}, u32[]{:S(2)}, u32[]{:S(2)}) async-start(bf16[8,2,6,16,256]{4,3,2,1,0:T(8,128)(2,1)} %collective-permute-done.4), calls=%async_computation.5 | async-start | bytes 1572864 | tf_op jit(solution)/shard_map/all_to_all | solution.py:352
  173.1 1.5 copy-done.10
  174.6 1.1 copy-done.13
  175.7 14.0 %shard_map.123 = (f32[2,384,256]{2,1,0:T(8,128)S(1)}, bf16[8,2,6,16,256]{4,3,2,1,0:T(8,128)(2,1)S(1)}) custom-call(bf16[256,256]{1,0:T(8,128)(2,1)S(1)} %select_convert_fusion.swap_ref, bf16[8,2,6,16,256]{4,3,2,1,0:T(8,128)(2,1)S(1)} %all-to-all-done.1.x_ref, bf16[2,384,48,256]{3,2,1,0:T(8,128)(2,1)} %bitcast.58, f32[2,384,256]{2,1,0:T(8,128)S(1)} %bitcast.53, ...), custom_call_target="tpu_custom_call" | custom-call | flops 20000000000 | bytes 6291456 | tf_op jit(solution)/shard_map/pallas_call | solution.py:123
  190.6 1.5 collective-permute-start.3
  192.1 14.7 %collective-permute-done.3 = bf16[8,2,6,16,256]{4,3,2,1,0:T(8,128)(2,1)S(1)} collective-permute-done((bf16[8,2,6,16,256]{4,3,2,1,0:T(8,128)(2,1)S(1)}, bf16[8,2,6,16,256]{4,3,2,1,0:T(8,128)(2,1)S(1)}, u32[]{:S(2)}, u32[]{:S(2)}) %collective-permute-start.3) | collective-permute-done | bytes 786464 | tf_op jit(solution)/shard_map/ppermute | solution.py:17
  206.8 0.9 copy-done.16
  207.7 5.7 %all-to-all-start.4 = ((bf16[8,2,6,16,256]{4,3,2,1,0:T(8,128)(2,1)}), bf16[8,2,6,16,256]{4,3,2,1,0:T(8,128)(2,1)S(1)}, u32[]{:S(2)}, u32[]{:S(2)}) async-start(bf16[8,2,6,16,256]{4,3,2,1,0:T(8,128)(2,1)} %copy-done.16), calls=%async_computation.4 | async-start | bytes 1572864 | tf_op jit(solution)/shard_map/all_to_all | solution.py:352
  213.4 1.7 add_convert_fusion.1
  216.0 13.5 %all-to-all-done.4.refs_1_ = bf16[8,2,6,16,256]{4,3,2,1,0:T(8,128)(2,1)S(1)} async-done(((bf16[8,2,6,16,256]{4,3,2,1,0:T(8,128)(2,1)}), bf16[8,2,6,16,256]{4,3,2,1,0:T(8,128)(2,1)S(1)}, u32[]{:S(2)}, u32[]{:S(2)}) %all-to-all-start.4) | async-done | bytes 786464 | tf_op jit(solution)/shard_map/all_to_all | solution.py:352
  229.4 4.1 %all-to-all-start.6 = ((bf16[2,8,48,256]{3,2,0,1:T(8,128)(2,1)}), bf16[2,8,48,256]{3,2,0,1:T(8,128)(2,1)}, u32[]{:S(2)}, u32[]{:S(2)}) async-start(bf16[2,8,48,256]{3,2,0,1:T(8,128)(2,1)} %copy.13), calls=%async_computation.6 | async-start | bytes 786432 | tf_op jit(solution)/shard_map/all_to_all | solution.py:357
  233.5 1.1 copy.14
  234.6 8.2 %all-to-all-done.6 = bf16[2,8,48,256]{3,2,0,1:T(8,128)(2,1)} async-done(((bf16[2,8,48,256]{3,2,0,1:T(8,128)(2,1)}), bf16[2,8,48,256]{3,2,0,1:T(8,128)(2,1)}, u32[]{:S(2)}, u32[]{:S(2)}) %all-to-all-start.6) | async-done | bytes 393248 | tf_op jit(solution)/shard_map/all_to_all | solution.py:357
  242.7 3.8 %all-to-all-start.7 = ((bf16[2,16,32,512]{3,2,0,1:T(8,128)(2,1)}), bf16[2,16,32,512]{3,2,0,1:T(8,128)(2,1)S(1)}, u32[]{:S(2)}, u32[]{:S(2)}) async-start(bf16[2,16,32,512]{3,2,0,1:T(8,128)(2,1)} %copy.14), calls=%async_computation.7 | async-start | bytes 2097152 | tf_op jit(solution)/shard_map/all_to_all | solution.py:360
  246.6 1.4 constant_dynamic-slice_fusion.table_ref
  247.9 3.1 %shard_map.124 = (bf16[6,384,256]{2,1,0:T(8,128)(2,1)S(1)}, bf16[6,384,256]{2,1,0:T(8,128)(2,1)S(1)}) custom-call(bf16[768,768]{1,0:T(8,128)(2,1)S(1)} %constant_dynamic-slice_fusion.table_ref, bf16[8,2,6,16,256]{4,3,2,1,0:T(8,128)(2,1)S(1)} %all-to-all-done.3.refs_0_, bf16[8,2,6,16,256]{4,3,2,1,0:T(8,128)(2,1)S(1)} %all-to-all-done.4.refs_1_, ...), custom_call_target="tpu_custom_call" | custom-call | tf_op jit(solution)/shard_map/pallas_call | solution.py:267
  251.5 1.7 convert_reduce_fusion.1
  254.1 3.7 %fusion = bf16[1,6,384,512]{3,2,1,0:T(8,128)(2,1)} fusion(bf16[6,384,512]{2,1,0:T(8,128)(2,1)} %collective-permute-done.2, bf16[6,384,256]{2,1,0:T(8,128)(2,1)S(1)} %get-tuple-element.49, bf16[6,384,256]{2,1,0:T(8,128)(2,1)S(1)} %get-tuple-element.48), kind=kLoop, calls=%fused_computation.1 | loop fusion | flops 8257536 | bytes 7077888 | tf_op jit(solution)/shard_map/broadcast_in_dim | solution.py:372
  257.8 11.7 %all-to-all-done.7 = bf16[2,16,32,512]{3,2,0,1:T(8,128)(2,1)S(1)} async-done(((bf16[2,16,32,512]{3,2,0,1:T(8,128)(2,1)}), bf16[2,16,32,512]{3,2,0,1:T(8,128)(2,1)S(1)}, u32[]{:S(2)}, u32[]{:S(2)}) %all-to-all-start.7) | async-done | bytes 1048608 | tf_op jit(solution)/shard_map/all_to_all | solution.py:360
  (36 shorter events, 7.1 us)
Async XLA Ops:
  0.6 1.7 copy-start
  2.3 1.7 copy-start.1
  4.0 1.0 copy-start.5
  5.0 1.0 copy-start.6
  16.4 1.4 copy-start.7
  17.8 6.2 %copy-start.15 = (bf16[6,384,256]{2,1,0:T(8,128)(2,1)}, bf16[6,384,256]{2,1,0:T(8,128)(2,1)S(1)}, u32[]{:S(2)}) copy-start(bf16[6,384,256]{2,1,0:T(8,128)(2,1)S(1)} %get-tuple-element.50) | copy-start | bytes 3538948
  17.8 3.1 %collective-permute-start = (bf16[6,384,256]{2,1,0:T(8,128)(2,1)S(1)}, bf16[6,384,256]{2,1,0:T(8,128)(2,1)}, u32[]{:S(2)}, u32[]{:S(2)}) collective-permute-start(bf16[6,384,256]{2,1,0:T(8,128)(2,1)S(1)} %get-tuple-element.51), channel_id=1, source_target_pairs={{1,0},{0,1},{3,2},{2,3},{5,4},{4,5},{7,6},{6,7},{9,8},{8,9},{11,10... | collective-permute-start | bytes 3538952 | tf_op jit(solution)/shard_map/ppermute | solution.py:17
  24.0 27.7 %all-to-all-start.2 = ((bf16[8,2,6,16,256]{4,3,2,1,0:T(8,128)(2,1)}), bf16[8,2,6,16,256]{4,3,2,1,0:T(8,128)(2,1)S(1)}, u32[]{:S(2)}, u32[]{:S(2)}) async-start(bf16[8,2,6,16,256]{4,3,2,1,0:T(8,128)(2,1)} %fusion.3), calls=%async_computation.2 | async-start | bytes 1572864 | tf_op jit(solution)/shard_map/all_to_all | solution.py:327
  51.6 24.0 %all-to-all-start.1 = ((bf16[8,2,6,16,256]{4,3,2,1,0:T(8,128)(2,1)}), bf16[8,2,6,16,256]{4,3,2,1,0:T(8,128)(2,1)S(1)}, u32[]{:S(2)}, u32[]{:S(2)}) async-start(bf16[8,2,6,16,256]{4,3,2,1,0:T(8,128)(2,1)} %fusion.2), calls=%async_computation.1 | async-start | bytes 1572864 | tf_op jit(solution)/shard_map/all_to_all | solution.py:327
  55.2 54.5 %collective-permute-start.2 = (bf16[6,384,512]{2,1,0:T(8,128)(2,1)}, bf16[6,384,512]{2,1,0:T(8,128)(2,1)}, u32[]{:S(2)}, u32[]{:S(2)}) collective-permute-start(bf16[6,384,512]{2,1,0:T(8,128)(2,1)} %copy-done.7), channel_id=1, source_target_pairs={{16,0},{0,16},{17,1},{1,17},{18,2},{2,18},{19,3},{3,19},{20,4},{4,... | collective-permute-start | bytes 7077896 | tf_op jit(solution)/shard_map/ppermute | solution.py:17
  75.6 34.1 %all-to-all-start = ((bf16[8,2,6,16,256]{4,3,2,1,0:T(8,128)(2,1)}), bf16[8,2,6,16,256]{4,3,2,1,0:T(8,128)(2,1)S(1)}, u32[]{:S(2)}, u32[]{:S(2)}) async-start(bf16[8,2,6,16,256]{4,3,2,1,0:T(8,128)(2,1)} %fusion.1), calls=%async_computation | async-start | bytes 1572864 | tf_op jit(solution)/shard_map/all_to_all | solution.py:327
  79.2 1.5 copy-start.8
  80.7 1.1 copy-start.11
  96.7 0.9 copy-start.2
  97.6 27.7 %collective-permute-start.1 = (bf16[8,2,6,16,256]{4,3,2,1,0:T(8,128)(2,1)}, bf16[8,2,6,16,256]{4,3,2,1,0:T(8,128)(2,1)}, u32[]{:S(2)}, u32[]{:S(2)}) collective-permute-start(bf16[8,2,6,16,256]{4,3,2,1,0:T(8,128)(2,1)} %get-tuple-element.29), channel_id=1, source_target_pairs={{16,0},{0,16},{17,1},{1,17},{18,2},{2,18},{19,3},{3,19},{20,4},{4,... | collective-permute-start | bytes 2359304 | tf_op jit(solution)/shard_map/ppermute | solution.py:17
  125.3 24.7 %all-to-all-start.3 = ((bf16[8,2,6,16,256]{4,3,2,1,0:T(8,128)(2,1)}), bf16[8,2,6,16,256]{4,3,2,1,0:T(8,128)(2,1)S(1)}, u32[]{:S(2)}, u32[]{:S(2)}) async-start(bf16[8,2,6,16,256]{4,3,2,1,0:T(8,128)(2,1)} %collective-permute-done.1), calls=%async_computation.3 | async-start | bytes 1572864 | tf_op jit(solution)/shard_map/all_to_all | solution.py:342
  131.0 1.5 copy-start.9
  132.5 1.1 copy-start.12
  147.6 0.9 copy-start.3
  148.5 0.9 copy-start.14
  150.0 17.5 %collective-permute-start.4 = (bf16[8,2,6,16,256]{4,3,2,1,0:T(8,128)(2,1)}, bf16[8,2,6,16,256]{4,3,2,1,0:T(8,128)(2,1)}, u32[]{:S(2)}, u32[]{:S(2)}) collective-permute-start(bf16[8,2,6,16,256]{4,3,2,1,0:T(8,128)(2,1)} %copy-done.14), channel_id=1, source_target_pairs={{16,0},{0,16},{17,1},{1,17},{18,2},{2,18},{19,3},{3,19},{20,4},{4,... | collective-permute-start | bytes 2359304 | tf_op jit(solution)/shard_map/ppermute | solution.py:17
  167.4 40.3 %all-to-all-start.5 = ((bf16[8,2,6,16,256]{4,3,2,1,0:T(8,128)(2,1)}), bf16[8,2,6,16,256]{4,3,2,1,0:T(8,128)(2,1)S(1)}, u32[]{:S(2)}, u32[]{:S(2)}) async-start(bf16[8,2,6,16,256]{4,3,2,1,0:T(8,128)(2,1)} %collective-permute-done.4), calls=%async_computation.5 | async-start | bytes 1572864 | tf_op jit(solution)/shard_map/all_to_all | solution.py:352
  173.1 1.5 copy-start.10
  174.6 1.1 copy-start.13
  189.7 0.9 copy-start.4
  190.6 16.2 %collective-permute-start.3 = (bf16[8,2,6,16,256]{4,3,2,1,0:T(8,128)(2,1)S(1)}, bf16[8,2,6,16,256]{4,3,2,1,0:T(8,128)(2,1)S(1)}, u32[]{:S(2)}, u32[]{:S(2)}) collective-permute-start(bf16[8,2,6,16,256]{4,3,2,1,0:T(8,128)(2,1)S(1)} %get-tuple-element.37), channel_id=1, source_target_pairs={{16,0},{0,16},{17,1},{1,17},{18,2},{2,18},{19,3},{3,19},{20,4},{4,... | collective-permute-start | bytes 2359304 | tf_op jit(solution)/shard_map/ppermute | solution.py:17
  206.8 0.9 copy-start.16
  207.7 21.7 %all-to-all-start.4 = ((bf16[8,2,6,16,256]{4,3,2,1,0:T(8,128)(2,1)}), bf16[8,2,6,16,256]{4,3,2,1,0:T(8,128)(2,1)S(1)}, u32[]{:S(2)}, u32[]{:S(2)}) async-start(bf16[8,2,6,16,256]{4,3,2,1,0:T(8,128)(2,1)} %copy-done.16), calls=%async_computation.4 | async-start | bytes 1572864 | tf_op jit(solution)/shard_map/all_to_all | solution.py:352
  229.4 13.3 %all-to-all-start.6 = ((bf16[2,8,48,256]{3,2,0,1:T(8,128)(2,1)}), bf16[2,8,48,256]{3,2,0,1:T(8,128)(2,1)}, u32[]{:S(2)}, u32[]{:S(2)}) async-start(bf16[2,8,48,256]{3,2,0,1:T(8,128)(2,1)} %copy.13), calls=%async_computation.6 | async-start | bytes 786432 | tf_op jit(solution)/shard_map/all_to_all | solution.py:357
  242.7 26.8 %all-to-all-start.7 = ((bf16[2,16,32,512]{3,2,0,1:T(8,128)(2,1)}), bf16[2,16,32,512]{3,2,0,1:T(8,128)(2,1)S(1)}, u32[]{:S(2)}, u32[]{:S(2)}) async-start(bf16[2,16,32,512]{3,2,0,1:T(8,128)(2,1)} %copy.14), calls=%async_computation.7 | async-start | bytes 2097152 | tf_op jit(solution)/shard_map/all_to_all | solution.py:360
  251.0 2.9 %collective-permute-start.5 = (bf16[6,384,256]{2,1,0:T(8,128)(2,1)S(1)}, bf16[6,384,256]{2,1,0:T(8,128)(2,1)S(1)}, u32[]{:S(2)}, u32[]{:S(2)}) collective-permute-start(bf16[6,384,256]{2,1,0:T(8,128)(2,1)S(1)} %get-tuple-element.45), channel_id=1, source_target_pairs={{1,0},{0,1},{3,2},{2,3},{5,4},{4,5},{7,6},{6,7},{9,8},{8,9},{11,10... | collective-permute-start | bytes 3538952 | tf_op jit(solution)/shard_map/ppermute | solution.py:17

commit v3 on v2

--- a/solution.py
+++ b/solution.py
@@ -294,7 +294,6 @@
     grad_grid, low, high, mixer_terms = mixer(
         block_hidden[0], incoming_grad[0], up_weight[0], down_weight[0]
     )
-    group_count = lax.axis_size(("lat", "lon"))
     lat_count = lax.axis_size("lat")
     lon_index = lax.axis_index("lon")
     half = embed // 2
@@ -319,46 +318,66 @@
     all_rows = jnp.concatenate([own, theirs], axis=1)
     synthesis = rolled(by_group(synthesis))
     analysis = rolled(by_group(analysis).reshape(period, -1))
-    bands, filter_terms = [], 0.0
+    unit_half = mixer_terms.shape[2] // 2
+    mixer_terms = mixer_terms.reshape(2, lat_count, 2, -1, 2 * unit_half)
+    mixer_other = jnp.where(lon_index == 0, mixer_terms[:, :, 1], mixer_terms[:, :, 0])
+    mixer_own = jnp.where(lon_index == 0, mixer_terms[:, :, 0], mixer_terms[:, :, 1])
+    mixer_theirs = shifted(mixer_other, "lon", 1)
+
+    def spread(block):
+        return lax.all_to_all(block, "lat", split_axis=0, concat_axis=0, tiled=True)
+
+    def run(group, block):
+        return (middle if fits else middle_plain)(
+            group, block, saved_coeffs[0], filter_weights[0], latitude_maps
+        )
+
+    def ordered(*values):
+        return lax.optimization_barrier(values)
+
+    spectra = []
     for group in range(groups):
-        spectrum = jnp.einsum(
-            "tkc,kdrj->drtjc", all_rows, synthesis[:, group], preferred_element_type=jnp.float32
-        ).astype(jnp.bfloat16)
-        bands.append(lax.all_to_all(spectrum, "lat", split_axis=0, concat_axis=0, tiled=True))
-    returned = []
-    flipped = []
+        spectra.append(
+            jnp.einsum(
+                "tkc,kdrj->drtjc", all_rows, synthesis[:, group], preferred_element_type=jnp.float32
+            ).astype(jnp.bfloat16)
+        )
+    arriving = [spread(block) for block in spectra[:2]]
+    filter_terms, flipped, returned = 0.0, [], []
     for group in range(groups):
         if group == 1:
-            bands[1], last_bands = lax.optimization_barrier((bands[1], back_bands))
-            back_bands = last_bands
+            arriving[1], handed_rows = ordered(arriving[1], handed_rows)
+        terms, out = run(group, arriving[group])
+        filter_terms = filter_terms + terms
+        if group + 2 < groups:
+            block, out = ordered(spectra[group + 2], out)
+            arriving.append(spread(block))
+        if group + 1 < groups:
+            arriving[group + 1], out = ordered(arriving[group + 1], out)
         if group >= 1:
-            flipped.append(shifted(back_bands, "section", 1))
-        if group == 2:
-            bands[2], flipped[0], handed_rows = lax.optimization_barrier(
-                (bands[2], flipped[0], handed_rows)
-            )
-        if group >= 2:
-            returned.append(
-                lax.all_to_all(flipped[group - 2], "lat", split_axis=0, concat_axis=0, tiled=True)
-            )
-        terms, back_bands = (middle if fits else middle_plain)(
-            group, bands[group], saved_coeffs[0], filter_weights[0], latitude_maps
-        )
-        filter_terms = filter_terms + terms
+            flipped[-1], out = ordered(flipped[-1], out)
+            if returned:
+                flipped[-1], returned[-1] = ordered(flipped[-1], returned[-1])
+            returned.append(spread(flipped[-1]))
+        flipped.append(shifted(out, "section", 1))
     if returned:
-        back_bands, returned[-1] = lax.optimization_barrier((back_bands, returned[-1]))
-    flipped.append(shifted(back_bands, "section", 1))
-    for block in flipped[len(returned) :]:
-        returned.append(lax.all_to_all(block, "lat", split_axis=0, concat_axis=0, tiled=True))
+        flipped[-1], returned[-1] = ordered(flipped[-1], returned[-1])
+    returned.append(spread(flipped[-1]))
+    mixer_sum = (mixer_own.astype(jnp.float32) + mixer_theirs.astype(jnp.float32)).astype(
+        jnp.bfloat16
+    )
+    mixer_sum = jnp.swapaxes(mixer_sum, 0, 1).reshape(lat_count, -1, 2 * unit_half)
+    share = mixer_sum.shape[1]
     filter_terms = filter_terms.reshape(2, lat_count, -1, half).astype(jnp.bfloat16)
-    mixer_terms, filter_terms, returned[-1] = lax.optimization_barrier(
-        (mixer_terms, filter_terms, returned[-1])
-    )
-    filter_parts = lax.all_to_all(filter_terms, "lat", split_axis=1, concat_axis=1, tiled=True)
-    filter_grad = jnp.sum(filter_parts.astype(jnp.float32), axis=1)
-    mixer_terms = mixer_terms.reshape(2, group_count, -1, mixer_terms.shape[2])
-    mixer_parts = lax.all_to_all(mixer_terms, ("lat", "lon"), split_axis=1, concat_axis=1, tiled=True)
-    up_grad, down_grad = jnp.sum(mixer_parts.astype(jnp.float32), axis=1)
+    filter_terms = jnp.swapaxes(filter_terms, 0, 1).reshape(lat_count, -1, half)
+    totals = jnp.concatenate(
+        [mixer_sum[..., :unit_half], mixer_sum[..., unit_half:], filter_terms], axis=1
+    )
+    totals, returned[-1] = ordered(totals, returned[-1])
+    totals = jnp.sum(spread(totals).astype(jnp.float32), axis=0)
+    mixer_total = jnp.concatenate([totals[:share], totals[share : 2 * share]], axis=1)
+    up_grad, down_grad = mixer_total[: share // 2], mixer_total[share // 2 :]
+    filter_grad = totals[2 * share :].reshape(2, -1, half)
     own_back, for_other = (back if fits else back_plain)(analysis, returned)
     their_back = shifted(for_other, "lon", 1)
     grid_back = jnp.concatenate(

time: 273 us -> 217 us (0.79)
  waiting for transfers between devices: 126 us -> 74.9 us
  starting transfers between devices: 46.3 us -> 42.2 us
    ppermute x6 -> x7, waiting for transfers between devices: 60.3 us -> 25.2 us  [shifted(): return lax.ppermute(block, axis, route)]
    all_to_all x8 -> x7, waiting for transfers between devices: 66 us -> 49.8 us  [spread(): return lax.all_to_all(block, 'lat', split_axis=0, concat_axis=0, tiled=True)]
    all_to_all x8 -> x7, starting transfers between devices: 39.4 us -> 36.6 us  [spread(): return lax.all_to_all(block, 'lat', split_axis=0, concat_axis=0, tiled=True)]
    ppermute x6 -> x7, starting transfers between devices: 6.95 us -> 5.64 us  [shifted(): return lax.ppermute(block, axis, route)]
    unnamed x34 -> x56, local copies, waits for them, and re-layouts: 18.9 us -> 19.4 us
  transfers between devices with their start and end apart: 14 -> 14, of which waited for: 12 -> 8; matrix products, arithmetic and copies ran while one was open for 7% -> 7% of each run, Pallas kernels for 17% -> 19%
where the time goes in v3:
time: 217 us; the launch traced here: 216 us
  waiting for transfers between devices  74.9 us (35%)
  Pallas kernels  56.4 us (26%)
  starting transfers between devices  42.2 us (19%)
  local copies, waits for them, and re-layouts  21.6 us (10%)
  other arithmetic  9.84 us (5%)
  matrix products  9.68 us (4%)
    all_to_all x7, waiting for transfers between devices, spread(): return lax.all_to_all(block, 'lat', split_axis=0, concat_axis=0, tiled=True)  49.8 us
    pallas_call x3, Pallas kernels, middle(): pl.pallas_call(middle_kernel, grid=(steps,), in_specs=[pl.BlockSpec((GROU...  42 us
    all_to_all x7, starting transfers between devices, spread(): return lax.all_to_all(block, 'lat', split_axis=0, concat_axis=0, tiled=True)  36.6 us
    ppermute x7, waiting for transfers between devices, shifted(): return lax.ppermute(block, axis, route)  25.2 us
    unnamed x56, local copies, waits for them, and re-layouts  19.4 us
    pallas_call x1, Pallas kernels, mixer(): pl.pallas_call(mixer_kernel, grid=(lats,), in_specs=[rows, rows, pl.Block...  10.3 us
    dot_general x3, matrix products, shards(): jnp.einsum('tkc,kdrj->drtjc', all_rows, synthesis[:, group], preferred_el...  9.68 us
    ppermute x7, starting transfers between devices, shifted(): return lax.ppermute(block, axis, route)  5.64 us
  transfers between devices with their start and end apart: 14, of which 8 were waited for; matrix products, arithmetic and copies ran while one was open for 7% of the time, Pallas kernels for 19%

profile of v3, /device:TPU:0, one launch (start us, length us, event | category | flops | bytes accessed | tf_op | source)
XLA Modules:
  0.0 215.7 jit_solution(4088982910243763847)
XLA Ops:
  0.6 1.7 copy-done
  2.3 1.7 copy-done.1
  4.0 1.0 copy-done.10
  5.0 1.0 copy-done.11
  6.1 10.3 %shard_map.120 = (bf16[6,384,512]{2,1,0:T(8,128)(2,1)S(1)}, bf16[6,384,256]{2,1,0:T(8,128)(2,1)S(1)}, bf16[6,384,256]{2,1,0:T(8,128)(2,1)S(1)}, bf16[2,512,512]{2,1,0:T(8,128)(2,1)S(1)}) custom-call(bf16[6,384,512]{2,1,0:T(8,128)(2,1)S(1)} %bitcast.58, bf16[6,384,512]{2,1,0:T(8,128)(2,1)S(1)} %bitcast.59, bf16[512,512]{1,0:T(8,128)(2,1)S(1)} %bitcast.61, ...), custom_call_target="tpu_custom_call" | custom-call | tf_op jit(solution)/shard_map/pallas_call | solution.py:222
  16.4 1.3 broadcast_select_fusion.3
  18.7 2.8 %collective-permute-done = bf16[6,384,256]{2,1,0:T(8,128)(2,1)} collective-permute-done((bf16[6,384,256]{2,1,0:T(8,128)(2,1)}, bf16[6,384,256]{2,1,0:T(8,128)(2,1)}, u32[]{:S(2)}, u32[]{:S(2)}) %collective-permute-start) | collective-permute-done | bytes 1179680 | tf_op jit(solution)/shard_map/ppermute | solution.py:17
  21.5 3.1 %fusion.3 = bf16[8,2,6,16,256]{4,3,2,1,0:T(8,128)(2,1)} fusion(bf16[6,384,256]{2,1,0:T(8,128)(2,1)} %collective-permute-done, bf16[6,384,256]{2,1,0:T(8,128)(2,1)S(1)} %get-tuple-element.66, bf16[1152,3,8,2,16]{0,4,3,2,1:T(8,128)(2,1)} %constant.59.clone, s32[]{:T(128)S(6)} %select_n.76), kind=kOutput, calls=%fused_computation.9 | convolution fusion | flops 609091584 | bytes 3538948 | tf_op jit(solution)/shard_map/tkc,kdrj->drtjc/dot_general | solution.py:341
  24.6 7.2 %all-to-all-start.1 = ((bf16[8,2,6,16,256]{4,3,2,1,0:T(8,128)(2,1)}), bf16[8,2,6,16,256]{4,3,2,1,0:T(8,128)(2,1)S(1)}, u32[]{:S(2)}, u32[]{:S(2)}) async-start(bf16[8,2,6,16,256]{4,3,2,1,0:T(8,128)(2,1)} %fusion.3), calls=%async_computation.1 | async-start | bytes 1572864 | tf_op jit(solution)/shard_map/all_to_all | solution.py:328
  31.8 1.5 collective-permute-start.1
  33.6 3.1 %fusion.2 = bf16[8,2,6,16,256]{4,3,2,1,0:T(8,128)(2,1)} fusion(bf16[6,384,256]{2,1,0:T(8,128)(2,1)} %collective-permute-done, bf16[6,384,256]{2,1,0:T(8,128)(2,1)S(1)} %get-tuple-element.66, bf16[1152,3,8,2,16]{0,4,3,2,1:T(8,128)(2,1)} %constant.59.clone, s32[]{:T(128)S(6)} %select_n.76, s32[]{:T(128)S(6)} %add.50), kind=kOutput, calls=%fused_computation.8 | convolution fusion | flops 609091584 | bytes 3538952 | tf_op jit(solution)/shard_map/tkc,kdrj->drtjc/dot_general | solution.py:341
  36.7 3.5 %fusion.1 = bf16[8,2,6,16,256]{4,3,2,1,0:T(8,128)(2,1)} fusion(bf16[6,384,256]{2,1,0:T(8,128)(2,1)} %collective-permute-done, bf16[6,384,256]{2,1,0:T(8,128)(2,1)} %copy-done.27, bf16[1152,3,8,2,16]{0,4,3,2,1:T(8,128)(2,1)} %constant.59.clone, s32[]{:T(128)S(6)} %select_n.76, s32[]{:T(128)S(6)} %add.49), kind=kOutput, calls=%fused_computation.7 | convolution fusion | flops 609091584 | bytes 3538952 | tf_op jit(solution)/shard_map/tkc,kdrj->drtjc/dot_general | solution.py:341
  40.2 12.0 %all-to-all-done.1.x_ref = bf16[8,2,6,16,256]{4,3,2,1,0:T(8,128)(2,1)S(1)} async-done(((bf16[8,2,6,16,256]{4,3,2,1,0:T(8,128)(2,1)}), bf16[8,2,6,16,256]{4,3,2,1,0:T(8,128)(2,1)S(1)}, u32[]{:S(2)}, u32[]{:S(2)}) %all-to-all-start.1) | async-done | bytes 786464 | tf_op jit(solution)/shard_map/all_to_all | solution.py:328
  52.2 3.6 %all-to-all-start = ((bf16[8,2,6,16,256]{4,3,2,1,0:T(8,128)(2,1)}), bf16[8,2,6,16,256]{4,3,2,1,0:T(8,128)(2,1)S(1)}, u32[]{:S(2)}, u32[]{:S(2)}) async-start(bf16[8,2,6,16,256]{4,3,2,1,0:T(8,128)(2,1)} %fusion.1), calls=%async_computation | async-start | bytes 1572864 | tf_op jit(solution)/shard_map/all_to_all | solution.py:328
  55.8 1.5 copy-done.15
  57.3 14.0 %shard_map.121 = (f32[2,384,256]{2,1,0:T(8,128)S(1)}, bf16[8,2,6,16,256]{4,3,2,1,0:T(8,128)(2,1)S(1)}) custom-call(bf16[256,256]{1,0:T(8,128)(2,1)S(1)} %select_convert_fusion.swap_ref, bf16[8,2,6,16,256]{4,3,2,1,0:T(8,128)(2,1)S(1)} %all-to-all-done.1.x_ref, bf16[2,384,48,256]{3,2,1,0:T(8,128)(2,1)} %bitcast.73, f32[2,384,256]{2,1,0:T(8,128)S(1)} %bitcast.66, ...), custom_call_target="tpu_custom_call" | custom-call | flops 20000000000 | bytes 6291456 | tf_op jit(solution)/shard_map/pallas_call | solution.py:123
  71.3 0.9 copy-done.4
  72.2 0.9 copy-done.21
  73.1 3.1 %all-to-all-done.x_ref = bf16[8,2,6,16,256]{4,3,2,1,0:T(8,128)(2,1)S(1)} async-done(((bf16[8,2,6,16,256]{4,3,2,1,0:T(8,128)(2,1)}), bf16[8,2,6,16,256]{4,3,2,1,0:T(8,128)(2,1)S(1)}, u32[]{:S(2)}, u32[]{:S(2)}) %all-to-all-start) | async-done | bytes 786464 | tf_op jit(solution)/shard_map/all_to_all | solution.py:328
  76.2 8.9 %collective-permute-done.1 = bf16[6,384,512]{2,1,0:T(8,128)(2,1)} collective-permute-done((bf16[6,384,512]{2,1,0:T(8,128)(2,1)}, bf16[6,384,512]{2,1,0:T(8,128)(2,1)}, u32[]{:S(2)}, u32[]{:S(2)}) %collective-permute-start.1) | collective-permute-done | bytes 2359328 | tf_op jit(solution)/shard_map/ppermute | solution.py:17
  85.1 5.7 %all-to-all-start.2 = ((bf16[8,2,6,16,256]{4,3,2,1,0:T(8,128)(2,1)}), bf16[8,2,6,16,256]{4,3,2,1,0:T(8,128)(2,1)S(1)}, u32[]{:S(2)}, u32[]{:S(2)}) async-start(bf16[8,2,6,16,256]{4,3,2,1,0:T(8,128)(2,1)} %fusion.2), calls=%async_computation.2 | async-start | bytes 1572864 | tf_op jit(solution)/shard_map/all_to_all | solution.py:328
  90.8 1.5 collective-permute-start.2
  92.3 1.5 copy-done.16
  93.8 1.1 copy-done.19
  94.9 14.0 %shard_map.122 = (f32[2,384,256]{2,1,0:T(8,128)S(1)}, bf16[8,2,6,16,256]{4,3,2,1,0:T(8,128)(2,1)S(1)}) custom-call(bf16[256,256]{1,0:T(8,128)(2,1)S(1)} %select_convert_fusion.swap_ref, bf16[8,2,6,16,256]{4,3,2,1,0:T(8,128)(2,1)S(1)} %all-to-all-done.x_ref, bf16[2,384,48,256]{3,2,1,0:T(8,128)(2,1)} %bitcast.74, f32[2,384,256]{2,1,0:T(8,128)S(1)} %bitcast.67, ...), custom_call_target="tpu_custom_call" | custom-call | flops 20000000000 | bytes 6291456 | tf_op jit(solution)/shard_map/pallas_call | solution.py:123
  108.9 0.9 copy-done.6
  109.8 0.9 copy-done.22
  111.4 5.8 %all-to-all-start.3 = ((bf16[8,2,6,16,256]{4,3,2,1,0:T(8,128)(2,1)}), bf16[8,2,6,16,256]{4,3,2,1,0:T(8,128)(2,1)S(1)}, u32[]{:S(2)}, u32[]{:S(2)}) async-start(bf16[8,2,6,16,256]{4,3,2,1,0:T(8,128)(2,1)} %collective-permute-done.2), calls=%async_computation.3 | async-start | bytes 1572864 | tf_op jit(solution)/shard_map/all_to_all | solution.py:328
  117.2 0.9 copy-done.13
  118.1 1.5 copy-done.17
  119.6 1.1 copy-done.20
  120.7 14.0 %shard_map.123 = (f32[2,384,256]{2,1,0:T(8,128)S(1)}, bf16[8,2,6,16,256]{4,3,2,1,0:T(8,128)(2,1)S(1)}) custom-call(bf16[256,256]{1,0:T(8,128)(2,1)S(1)} %copy-done.13, bf16[8,2,6,16,256]{4,3,2,1,0:T(8,128)(2,1)S(1)} %all-to-all-done.2.x_ref, bf16[2,384,48,256]{3,2,1,0:T(8,128)(2,1)} %bitcast.75, f32[2,384,256]{2,1,0:T(8,128)S(1)} %bitcast.68, ...), custom_call_target="tpu_custom_call" | custom-call | flops 20000000000 | bytes 6291456 | tf_op jit(solution)/shard_map/pallas_call | solution.py:123
  134.7 0.9 copy-done.8
  135.6 6.0 %all-to-all-start.4 = ((bf16[8,2,6,16,256]{4,3,2,1,0:T(8,128)(2,1)}), bf16[8,2,6,16,256]{4,3,2,1,0:T(8,128)(2,1)S(1)}, u32[]{:S(2)}, u32[]{:S(2)}) async-start(bf16[8,2,6,16,256]{4,3,2,1,0:T(8,128)(2,1)} %collective-permute-done.3), calls=%async_computation.4 | async-start | bytes 1572864 | tf_op jit(solution)/shard_map/all_to_all | solution.py:328
  141.6 1.5 collective-permute-start.4
  143.2 1.0 select_bitcast_fusion
  144.4 13.4 %collective-permute-done.4 = bf16[8,2,6,16,256]{4,3,2,1,0:T(8,128)(2,1)} collective-permute-done((bf16[8,2,6,16,256]{4,3,2,1,0:T(8,128)(2,1)S(1)}, bf16[8,2,6,16,256]{4,3,2,1,0:T(8,128)(2,1)}, u32[]{:S(2)}, u32[]{:S(2)}) %collective-permute-start.4) | collective-permute-done | bytes 786464 | tf_op jit(solution)/shard_map/ppermute | solution.py:17
  157.9 1.2 all-to-all-done.4.refs_1_
  159.0 4.6 %all-to-all-start.5 = ((bf16[8,2,6,16,256]{4,3,2,1,0:T(8,128)(2,1)}), bf16[8,2,6,16,256]{4,3,2,1,0:T(8,128)(2,1)S(1)}, u32[]{:S(2)}, u32[]{:S(2)}) async-start(bf16[8,2,6,16,256]{4,3,2,1,0:T(8,128)(2,1)} %collective-permute-done.4), calls=%async_computation.5 | async-start | bytes 1572864 | tf_op jit(solution)/shard_map/all_to_all | solution.py:328
  163.6 1.4 constant_dynamic-slice_fusion.table_ref
  165.2 1.4 fusion.4
  167.1 1.0 pad_maximum_fusion
  168.0 13.7 %all-to-all-done.5.refs_2_ = bf16[8,2,6,16,256]{4,3,2,1,0:T(8,128)(2,1)S(1)} async-done(((bf16[8,2,6,16,256]{4,3,2,1,0:T(8,128)(2,1)}), bf16[8,2,6,16,256]{4,3,2,1,0:T(8,128)(2,1)S(1)}, u32[]{:S(2)}, u32[]{:S(2)}) %all-to-all-start.5) | async-done | bytes 786464 | tf_op jit(solution)/shard_map/all_to_all | solution.py:328
  181.8 4.1 %shard_map.124 = (bf16[6,384,256]{2,1,0:T(8,128)(2,1)S(1)}, bf16[6,384,256]{2,1,0:T(8,128)(2,1)}) custom-call(bf16[768,768]{1,0:T(8,128)(2,1)S(1)} %constant_dynamic-slice_fusion.table_ref, bf16[8,2,6,16,256]{4,3,2,1,0:T(8,128)(2,1)S(1)} %all-to-all-done.3.refs_0_, bf16[8,2,6,16,256]{4,3,2,1,0:T(8,128)(2,1)S(1)} %all-to-all-done.4.refs_1_, ...), custom_call_target="tpu_custom_call" | custom-call | tf_op jit(solution)/shard_map/pallas_call | solution.py:267
  185.8 1.0 copy-done.2
  186.9 3.7 %all-to-all-start.6 = ((bf16[8,224,256]{2,1,0:T(8,128)(2,1)}), bf16[8,224,256]{2,1,0:T(8,128)(2,1)S(1)}, u32[]{:S(2)}, u32[]{:S(2)}) async-start(bf16[8,224,256]{2,1,0:T(8,128)(2,1)} %pad_maximum_fusion), calls=%async_computation.6 | async-start | bytes 1835008 | tf_op jit(solution)/shard_map/all_to_all | solution.py:328
  190.7 3.7 %fusion = bf16[1,6,384,512]{3,2,1,0:T(8,128)(2,1)} fusion(bf16[6,384,512]{2,1,0:T(8,128)(2,1)} %collective-permute-done.1, bf16[6,384,256]{2,1,0:T(8,128)(2,1)S(1)} %get-tuple-element.65, bf16[6,384,256]{2,1,0:T(8,128)(2,1)S(1)} %get-tuple-element.64), kind=kLoop, calls=%fused_computation.1 | loop fusion | flops 8257536 | bytes 7077888 | tf_op jit(solution)/shard_map/broadcast_in_dim | solution.py:391
  194.4 19.8 %all-to-all-done.6 = bf16[8,224,256]{2,1,0:T(8,128)(2,1)S(1)} async-done(((bf16[8,224,256]{2,1,0:T(8,128)(2,1)}), bf16[8,224,256]{2,1,0:T(8,128)(2,1)S(1)}, u32[]{:S(2)}, u32[]{:S(2)}) %all-to-all-start.6) | async-done | bytes 917536 | tf_op jit(solution)/shard_map/all_to_all | solution.py:328
  (63 shorter events, 4.3 us)
Async XLA Ops:
  0.6 1.7 copy-start
  2.3 1.7 copy-start.1
  4.0 1.0 copy-start.10
  5.0 1.0 copy-start.11
  16.4 1.8 copy-start.14
  18.2 15.3 %copy-start.27 = (bf16[6,384,256]{2,1,0:T(8,128)(2,1)}, bf16[6,384,256]{2,1,0:T(8,128)(2,1)S(1)}, u32[]{:S(2)}) copy-start(bf16[6,384,256]{2,1,0:T(8,128)(2,1)S(1)} %get-tuple-element.66) | copy-start | bytes 3538948
  18.2 3.3 %collective-permute-start = (bf16[6,384,256]{2,1,0:T(8,128)(2,1)}, bf16[6,384,256]{2,1,0:T(8,128)(2,1)}, u32[]{:S(2)}, u32[]{:S(2)}) collective-permute-start(bf16[6,384,256]{2,1,0:T(8,128)(2,1)} %get-tuple-element.67), channel_id=1, source_target_pairs={{1,0},{0,1},{3,2},{2,3},{5,4},{4,5},{7,6},{6,7},{9,8},{8,9},{11,10... | collective-permute-start | bytes 3538952 | tf_op jit(solution)/shard_map/ppermute | solution.py:17
  24.6 27.6 %all-to-all-start.1 = ((bf16[8,2,6,16,256]{4,3,2,1,0:T(8,128)(2,1)}), bf16[8,2,6,16,256]{4,3,2,1,0:T(8,128)(2,1)S(1)}, u32[]{:S(2)}, u32[]{:S(2)}) async-start(bf16[8,2,6,16,256]{4,3,2,1,0:T(8,128)(2,1)} %fusion.3), calls=%async_computation.1 | async-start | bytes 1572864 | tf_op jit(solution)/shard_map/all_to_all | solution.py:328
  31.8 53.3 %collective-permute-start.1 = (bf16[6,384,512]{2,1,0:T(8,128)(2,1)}, bf16[6,384,512]{2,1,0:T(8,128)(2,1)}, u32[]{:S(2)}, u32[]{:S(2)}) collective-permute-start(bf16[6,384,512]{2,1,0:T(8,128)(2,1)} %copy-done.14), channel_id=1, source_target_pairs={{16,0},{0,16},{17,1},{1,17},{18,2},{2,18},{19,3},{3,19},{20,4},{4,... | collective-permute-start | bytes 7077896 | tf_op jit(solution)/shard_map/ppermute | solution.py:17
  33.6 58.7 %copy-start.12 = (bf16[256,256]{1,0:T(8,128)(2,1)}, bf16[256,256]{1,0:T(8,128)(2,1)S(1)}, u32[]{:S(2)}) copy-start(bf16[256,256]{1,0:T(8,128)(2,1)S(1)} %select_convert_fusion.swap_ref) | copy-start | bytes 393220
  36.7 19.1 %copy-start.18 = (f32[1,2,384,256]{3,2,1,0:T(8,128)S(1)}, f32[1,2,384,256]{3,2,1,0:T(8,128)}, u32[]{:S(2)}) copy-start(f32[1,2,384,256]{3,2,1,0:T(8,128)} %param.12) | copy-start | bytes 2359300
  52.2 24.0 %all-to-all-start = ((bf16[8,2,6,16,256]{4,3,2,1,0:T(8,128)(2,1)}), bf16[8,2,6,16,256]{4,3,2,1,0:T(8,128)(2,1)S(1)}, u32[]{:S(2)}, u32[]{:S(2)}) async-start(bf16[8,2,6,16,256]{4,3,2,1,0:T(8,128)(2,1)} %fusion.1), calls=%async_computation | async-start | bytes 1572864 | tf_op jit(solution)/shard_map/all_to_all | solution.py:328
  55.8 1.5 copy-start.15
  71.3 0.9 copy-start.4
  72.2 0.9 copy-start.21
  85.1 25.6 %all-to-all-start.2 = ((bf16[8,2,6,16,256]{4,3,2,1,0:T(8,128)(2,1)}), bf16[8,2,6,16,256]{4,3,2,1,0:T(8,128)(2,1)S(1)}, u32[]{:S(2)}, u32[]{:S(2)}) async-start(bf16[8,2,6,16,256]{4,3,2,1,0:T(8,128)(2,1)} %fusion.2), calls=%async_computation.2 | async-start | bytes 1572864 | tf_op jit(solution)/shard_map/all_to_all | solution.py:328
  90.8 19.9 %collective-permute-start.2 = (bf16[8,2,6,16,256]{4,3,2,1,0:T(8,128)(2,1)}, bf16[8,2,6,16,256]{4,3,2,1,0:T(8,128)(2,1)}, u32[]{:S(2)}, u32[]{:S(2)}) collective-permute-start(bf16[8,2,6,16,256]{4,3,2,1,0:T(8,128)(2,1)} %copy-done.21), channel_id=1, source_target_pairs={{16,0},{0,16},{17,1},{1,17},{18,2},{2,18},{19,3},{3,19},{20,4},{4,... | collective-permute-start | bytes 2359304 | tf_op jit(solution)/shard_map/ppermute | solution.py:17
  92.3 1.5 copy-start.16
  93.8 1.1 copy-start.19
  108.9 0.9 copy-start.6
  109.8 0.9 copy-start.22
  110.7 24.9 %collective-permute-start.3 = (bf16[8,2,6,16,256]{4,3,2,1,0:T(8,128)(2,1)}, bf16[8,2,6,16,256]{4,3,2,1,0:T(8,128)(2,1)}, u32[]{:S(2)}, u32[]{:S(2)}) collective-permute-start(bf16[8,2,6,16,256]{4,3,2,1,0:T(8,128)(2,1)} %copy-done.22), channel_id=1, source_target_pairs={{16,0},{0,16},{17,1},{1,17},{18,2},{2,18},{19,3},{3,19},{20,4},{4,... | collective-permute-start | bytes 2359304 | tf_op jit(solution)/shard_map/ppermute | solution.py:17
  111.4 24.3 %all-to-all-start.3 = ((bf16[8,2,6,16,256]{4,3,2,1,0:T(8,128)(2,1)}), bf16[8,2,6,16,256]{4,3,2,1,0:T(8,128)(2,1)S(1)}, u32[]{:S(2)}, u32[]{:S(2)}) async-start(bf16[8,2,6,16,256]{4,3,2,1,0:T(8,128)(2,1)} %collective-permute-done.2), calls=%async_computation.3 | async-start | bytes 1572864 | tf_op jit(solution)/shard_map/all_to_all | solution.py:328
  117.2 0.9 copy-start.13
  118.1 1.5 copy-start.17
  119.6 1.1 copy-start.20
  134.7 0.9 copy-start.8
  135.6 23.4 %all-to-all-start.4 = ((bf16[8,2,6,16,256]{4,3,2,1,0:T(8,128)(2,1)}), bf16[8,2,6,16,256]{4,3,2,1,0:T(8,128)(2,1)S(1)}, u32[]{:S(2)}, u32[]{:S(2)}) async-start(bf16[8,2,6,16,256]{4,3,2,1,0:T(8,128)(2,1)} %collective-permute-done.3), calls=%async_computation.4 | async-start | bytes 1572864 | tf_op jit(solution)/shard_map/all_to_all | solution.py:328
  141.6 16.3 %collective-permute-start.4 = (bf16[8,2,6,16,256]{4,3,2,1,0:T(8,128)(2,1)S(1)}, bf16[8,2,6,16,256]{4,3,2,1,0:T(8,128)(2,1)}, u32[]{:S(2)}, u32[]{:S(2)}) collective-permute-start(bf16[8,2,6,16,256]{4,3,2,1,0:T(8,128)(2,1)S(1)} %get-tuple-element.52), channel_id=1, source_target_pairs={{16,0},{0,16},{17,1},{1,17},{18,2},{2,18},{19,3},{3,19},{20,4},{4,... | collective-permute-start | bytes 2359304 | tf_op jit(solution)/shard_map/ppermute | solution.py:17
  143.2 1.0 copy-start.23
  143.2 1.2 copy-start.25
  144.2 20.9 %collective-permute-start.5 = (bf16[2,8,32,512]{3,2,0,1:T(8,128)(2,1)}, bf16[2,8,32,512]{3,2,0,1:T(8,128)(2,1)}, u32[]{:S(2)}, u32[]{:S(2)}) collective-permute-start(bf16[2,8,32,512]{3,2,0,1:T(8,128)(2,1)} %select_bitcast_fusion), channel_id=1, source_target_pairs={{1,0},{0,1},{3,2},{2,3},{5,4},{4,5},{7,6},{6,7},{9,8},{8,9},{11,10... | collective-permute-start | bytes 1572872 | tf_op jit(solution)/shard_map/ppermute | solution.py:17
  159.0 22.7 %all-to-all-start.5 = ((bf16[8,2,6,16,256]{4,3,2,1,0:T(8,128)(2,1)}), bf16[8,2,6,16,256]{4,3,2,1,0:T(8,128)(2,1)S(1)}, u32[]{:S(2)}, u32[]{:S(2)}) async-start(bf16[8,2,6,16,256]{4,3,2,1,0:T(8,128)(2,1)} %collective-permute-done.4), calls=%async_computation.5 | async-start | bytes 1572864 | tf_op jit(solution)/shard_map/all_to_all | solution.py:328
  163.6 1.5 copy-start.24
  163.6 1.6 copy-start.26
  165.1 1.6 copy-start.5
  165.1 1.6 copy-start.7
  165.1 1.8 copy-start.9
  185.8 1.0 copy-start.2
  186.8 3.7 %copy-start.3 = (bf16[6,384,256]{2,1,0:T(8,128)(2,1)S(1)}, bf16[6,384,256]{2,1,0:T(8,128)(2,1)}, u32[]{:S(2)}) copy-start(bf16[6,384,256]{2,1,0:T(8,128)(2,1)} %copy-done.2) | copy-start | bytes 3538948
  186.8 3.7 %collective-permute-start.6 = (bf16[6,384,256]{2,1,0:T(8,128)(2,1)}, bf16[6,384,256]{2,1,0:T(8,128)(2,1)S(1)}, u32[]{:S(2)}, u32[]{:S(2)}) collective-permute-start(bf16[6,384,256]{2,1,0:T(8,128)(2,1)} %get-tuple-element.62), channel_id=1, source_target_pairs={{1,0},{0,1},{3,2},{2,3},{5,4},{4,5},{7,6},{6,7},{9,8},{8,9},{11,10... | collective-permute-start | bytes 3538952 | tf_op jit(solution)/shard_map/ppermute | solution.py:17
  186.9 27.4 %all-to-all-start.6 = ((bf16[8,224,256]{2,1,0:T(8,128)(2,1)}), bf16[8,224,256]{2,1,0:T(8,128)(2,1)S(1)}, u32[]{:S(2)}, u32[]{:S(2)}) async-start(bf16[8,224,256]{2,1,0:T(8,128)(2,1)} %pad_maximum_fusion), calls=%async_computation.6 | async-start | bytes 1835008 | tf_op jit(solution)/shard_map/all_to_all | solution.py:328

commit v4 on v3

--- a/solution.py
+++ b/solution.py
@@ -335,6 +335,12 @@
     def ordered(*values):
         return lax.optimization_barrier(values)
 
+    mixer_sum = (mixer_own.astype(jnp.float32) + mixer_theirs.astype(jnp.float32)).astype(
+        jnp.bfloat16
+    )
+    mixer_sum = jnp.swapaxes(mixer_sum, 0, 1).reshape(lat_count, -1, 2 * unit_half)
+    share = mixer_sum.shape[1]
+    mixer_sum = jnp.concatenate([mixer_sum[..., :unit_half], mixer_sum[..., unit_half:]], axis=1)
     spectra = []
     for group in range(groups):
         spectra.append(
@@ -349,8 +355,13 @@
             arriving[1], handed_rows = ordered(arriving[1], handed_rows)
         terms, out = run(group, arriving[group])
         filter_terms = filter_terms + terms
+        if group == 0:
+            mixer_sum, arriving[-1], out = ordered(mixer_sum, arriving[-1], out)
+            mixer_parts = spread(mixer_sum)
         if group + 2 < groups:
             block, out = ordered(spectra[group + 2], out)
+            if group == 0:
+                block, mixer_parts = ordered(block, mixer_parts)
             arriving.append(spread(block))
         if group + 1 < groups:
             arriving[group + 1], out = ordered(arriving[group + 1], out)
@@ -363,21 +374,13 @@
     if returned:
         flipped[-1], returned[-1] = ordered(flipped[-1], returned[-1])
     returned.append(spread(flipped[-1]))
-    mixer_sum = (mixer_own.astype(jnp.float32) + mixer_theirs.astype(jnp.float32)).astype(
-        jnp.bfloat16
-    )
-    mixer_sum = jnp.swapaxes(mixer_sum, 0, 1).reshape(lat_count, -1, 2 * unit_half)
-    share = mixer_sum.shape[1]
     filter_terms = filter_terms.reshape(2, lat_count, -1, half).astype(jnp.bfloat16)
     filter_terms = jnp.swapaxes(filter_terms, 0, 1).reshape(lat_count, -1, half)
-    totals = jnp.concatenate(
-        [mixer_sum[..., :unit_half], mixer_sum[..., unit_half:], filter_terms], axis=1
-    )
-    totals, returned[-1] = ordered(totals, returned[-1])
-    totals = jnp.sum(spread(totals).astype(jnp.float32), axis=0)
-    mixer_total = jnp.concatenate([totals[:share], totals[share : 2 * share]], axis=1)
+    filter_terms, returned[-1] = ordered(filter_terms, returned[-1])
+    filter_grad = jnp.sum(spread(filter_terms).astype(jnp.float32), axis=0).reshape(2, -1, half)
+    totals = jnp.sum(mixer_parts.astype(jnp.float32), axis=0)
+    mixer_total = jnp.concatenate([totals[:share], totals[share:]], axis=1)
     up_grad, down_grad = mixer_total[: share // 2], mixer_total[share // 2 :]
-    filter_grad = totals[2 * share :].reshape(2, -1, half)
     own_back, for_other = (back if fits else back_plain)(analysis, returned)
     their_back = shifted(for_other, "lon", 1)
     grid_back = jnp.concatenate(

time: 217 us -> 219 us (level)
  waiting for transfers between devices: 74.9 us -> 79.8 us
  local copies, waits for them, and re-layouts: 21.6 us -> 17.7 us
  Pallas kernels: 56.4 us -> 59 us
  starting transfers between devices: 42.2 us -> 39.8 us
    all_to_all x7 -> x8, waiting for transfers between devices: 49.8 us -> 55.8 us  [spread(): return lax.all_to_all(block, 'lat', split_axis=0, concat_axis=0, tiled=True)]
    unnamed x56 -> x36, local copies, waits for them, and re-layouts: 19.4 us -> 15.4 us
    all_to_all x7 -> x8, starting transfers between devices: 36.6 us -> 34.2 us  [spread(): return lax.all_to_all(block, 'lat', split_axis=0, concat_axis=0, tiled=True)]
  transfers between devices with their start and end apart: 14 -> 15, of which waited for: 8 -> 11; matrix products, arithmetic and copies ran while one was open for 7% -> 7% of each run, Pallas kernels for 19% -> 20%
where the time goes in v4:
time: 219 us; the launch traced here: 217 us
  waiting for transfers between devices  79.8 us (36%)
  Pallas kernels  59 us (27%)
  starting transfers between devices  39.8 us (18%)
  local copies, waits for them, and re-layouts  17.7 us (8%)
  other arithmetic  10.7 us (5%)
  matrix products  9.63 us (4%)
    all_to_all x8, waiting for transfers between devices, spread(): return lax.all_to_all(block, 'lat', split_axis=0, concat_axis=0, tiled=True)  55.8 us
    pallas_call x3, Pallas kernels, middle(): pl.pallas_call(middle_kernel, grid=(steps,), in_specs=[pl.BlockSpec((GROU...  43.8 us
    all_to_all x8, starting transfers between devices, spread(): return lax.all_to_all(block, 'lat', split_axis=0, concat_axis=0, tiled=True)  34.2 us
    ppermute x7, waiting for transfers between devices, shifted(): return lax.ppermute(block, axis, route)  24 us
    unnamed x36, local copies, waits for them, and re-layouts  15.4 us
    pallas_call x1, Pallas kernels, mixer(): pl.pallas_call(mixer_kernel, grid=(lats,), in_specs=[rows, rows, pl.Block...  11.2 us
    dot_general x3, matrix products, shards(): jnp.einsum('tkc,kdrj->drtjc', all_rows, synthesis[:, group], preferred_el...  9.63 us
    ppermute x7, starting transfers between devices, shifted(): return lax.ppermute(block, axis, route)  5.61 us
  transfers between devices with their start and end apart: 15, of which 11 were waited for; matrix products, arithmetic and copies ran while one was open for 7% of the time, Pallas kernels for 20%

profile of v4, /device:TPU:0, one launch (start us, length us, event | category | flops | bytes accessed | tf_op | source)
XLA Modules:
  0.0 217.4 jit_solution(14807672079258718736)
XLA Ops:
  0.6 1.7 copy-done
  2.3 1.7 copy-done.1
  4.0 1.0 copy-done.7
  5.0 1.0 copy-done.8
  6.1 11.2 %shard_map.120 = (bf16[6,384,512]{2,1,0:T(8,128)(2,1)}, bf16[6,384,256]{2,1,0:T(8,128)(2,1)S(1)}, bf16[6,384,256]{2,1,0:T(8,128)(2,1)S(1)}, bf16[2,512,512]{2,1,0:T(8,128)(2,1)S(1)}) custom-call(bf16[6,384,512]{2,1,0:T(8,128)(2,1)S(1)} %bitcast.58, bf16[6,384,512]{2,1,0:T(8,128)(2,1)S(1)} %bitcast.59, bf16[512,512]{1,0:T(8,128)(2,1)S(1)} %bitcast.61, ...), custom_call_target="tpu_custom_call" | custom-call | tf_op jit(solution)/shard_map/pallas_call | solution.py:222
  17.2 1.2 broadcast_select_fusion.3
  19.0 2.7 %collective-permute-done.1 = bf16[6,384,256]{2,1,0:T(8,128)(2,1)} collective-permute-done((bf16[6,384,256]{2,1,0:T(8,128)(2,1)}, bf16[6,384,256]{2,1,0:T(8,128)(2,1)}, u32[]{:S(2)}, u32[]{:S(2)}) %collective-permute-start.1) | collective-permute-done | bytes 1179680 | tf_op jit(solution)/shard_map/ppermute | solution.py:17
  21.7 3.1 %fusion.2 = bf16[8,2,6,16,256]{4,3,2,1,0:T(8,128)(2,1)} fusion(bf16[6,384,256]{2,1,0:T(8,128)(2,1)} %collective-permute-done.1, bf16[6,384,256]{2,1,0:T(8,128)(2,1)S(1)} %get-tuple-element.76, bf16[1152,3,8,2,16]{0,4,3,2,1:T(8,128)(2,1)} %constant.59.clone, s32[]{:T(128)S(6)} %select_n.80), kind=kOutput, calls=%fused_computation.7 | convolution fusion | flops 609091584 | bytes 3538948 | tf_op jit(solution)/shard_map/tkc,kdrj->drtjc/dot_general | solution.py:347
  24.8 7.2 %all-to-all-start.1 = ((bf16[8,2,6,16,256]{4,3,2,1,0:T(8,128)(2,1)}), bf16[8,2,6,16,256]{4,3,2,1,0:T(8,128)(2,1)S(1)}, u32[]{:S(2)}, u32[]{:S(2)}) async-start(bf16[8,2,6,16,256]{4,3,2,1,0:T(8,128)(2,1)} %fusion.2), calls=%async_computation.1 | async-start | bytes 1572864 | tf_op jit(solution)/shard_map/all_to_all | solution.py:328
  32.1 1.6 collective-permute-start.2
  35.3 3.1 %fusion.1 = bf16[8,2,6,16,256]{4,3,2,1,0:T(8,128)(2,1)} fusion(bf16[6,384,256]{2,1,0:T(8,128)(2,1)} %collective-permute-done.1, bf16[6,384,256]{2,1,0:T(8,128)(2,1)S(1)} %copy-done.16, bf16[1152,3,8,2,16]{0,4,3,2,1:T(8,128)(2,1)} %constant.59.clone, s32[]{:T(128)S(6)} %select_n.80, s32[]{:T(128)S(6)} %add.49), kind=kOutput, calls=%fused_computation.6 | convolution fusion | flops 609091584 | bytes 3538952 | tf_op jit(solution)/shard_map/tkc,kdrj->drtjc/dot_general | solution.py:347
  38.4 14.1 %all-to-all-done.1.x_ref = bf16[8,2,6,16,256]{4,3,2,1,0:T(8,128)(2,1)S(1)} async-done(((bf16[8,2,6,16,256]{4,3,2,1,0:T(8,128)(2,1)}), bf16[8,2,6,16,256]{4,3,2,1,0:T(8,128)(2,1)S(1)}, u32[]{:S(2)}, u32[]{:S(2)}) %all-to-all-start.1) | async-done | bytes 786464 | tf_op jit(solution)/shard_map/all_to_all | solution.py:328
  52.5 3.6 %all-to-all-start = ((bf16[8,2,6,16,256]{4,3,2,1,0:T(8,128)(2,1)}), bf16[8,2,6,16,256]{4,3,2,1,0:T(8,128)(2,1)S(1)}, u32[]{:S(2)}, u32[]{:S(2)}) async-start(bf16[8,2,6,16,256]{4,3,2,1,0:T(8,128)(2,1)} %fusion.1), calls=%async_computation | async-start | bytes 1572864 | tf_op jit(solution)/shard_map/all_to_all | solution.py:328
  56.1 1.5 copy-done.9
  57.5 14.9 %shard_map.121 = (f32[2,384,256]{2,1,0:T(8,128)S(1)}, bf16[8,2,6,16,256]{4,3,2,1,0:T(8,128)(2,1)}) custom-call(bf16[256,256]{1,0:T(8,128)(2,1)S(1)} %select_convert_fusion.swap_ref, bf16[8,2,6,16,256]{4,3,2,1,0:T(8,128)(2,1)S(1)} %all-to-all-done.1.x_ref, bf16[2,384,48,256]{3,2,1,0:T(8,128)(2,1)} %bitcast.73, f32[2,384,256]{2,1,0:T(8,128)S(1)} %bitcast.66, ...), custom_call_target="tpu_custom_call" | custom-call | flops 20000000000 | bytes 6291456 | tf_op jit(solution)/shard_map/pallas_call | solution.py:123
  72.4 0.9 copy-done.4
  73.3 3.1 %all-to-all-done.x_ref = bf16[8,2,6,16,256]{4,3,2,1,0:T(8,128)(2,1)S(1)} async-done(((bf16[8,2,6,16,256]{4,3,2,1,0:T(8,128)(2,1)}), bf16[8,2,6,16,256]{4,3,2,1,0:T(8,128)(2,1)S(1)}, u32[]{:S(2)}, u32[]{:S(2)}) %all-to-all-start) | async-done | bytes 786464 | tf_op jit(solution)/shard_map/all_to_all | solution.py:328
  76.4 3.5 %all-to-all-start.2 = ((bf16[8,128,256]{2,1,0:T(8,128)(2,1)}), bf16[8,128,256]{2,1,0:T(8,128)(2,1)S(1)}, u32[]{:S(2)}, u32[]{:S(2)}) async-start(bf16[8,128,256]{2,1,0:T(8,128)(2,1)} %pad_maximum_fusion), calls=%async_computation.2 | async-start | bytes 1048576 | tf_op jit(solution)/shard_map/all_to_all | solution.py:328
  80.0 3.4 %fusion.3 = bf16[8,2,6,16,256]{4,3,2,1,0:T(8,128)(2,1)} fusion(bf16[6,384,256]{2,1,0:T(8,128)(2,1)} %collective-permute-done.1, bf16[6,384,256]{2,1,0:T(8,128)(2,1)} %copy-done.15, bf16[1152,3,8,2,16]{0,4,3,2,1:T(8,128)(2,1)} %constant.59.clone, s32[]{:T(128)S(6)} %select_n.80, s32[]{:T(128)S(6)} %add.50), kind=kOutput, calls=%fused_computation.8 | convolution fusion | flops 609091584 | bytes 3538952 | tf_op jit(solution)/shard_map/tkc,kdrj->drtjc/dot_general | solution.py:347
  83.4 2.7 %collective-permute-done.2 = bf16[6,384,512]{2,1,0:T(8,128)(2,1)} collective-permute-done((bf16[6,384,512]{2,1,0:T(8,128)(2,1)}, bf16[6,384,512]{2,1,0:T(8,128)(2,1)}, u32[]{:S(2)}, u32[]{:S(2)}) %collective-permute-start.2) | collective-permute-done | bytes 2359328 | tf_op jit(solution)/shard_map/ppermute | solution.py:17
  86.1 1.5 collective-permute-start.3
  87.6 7.0 %all-to-all-done.2 = bf16[8,128,256]{2,1,0:T(8,128)(2,1)S(1)} async-done(((bf16[8,128,256]{2,1,0:T(8,128)(2,1)}), bf16[8,128,256]{2,1,0:T(8,128)(2,1)S(1)}, u32[]{:S(2)}, u32[]{:S(2)}) %all-to-all-start.2) | async-done | bytes 524320 | tf_op jit(solution)/shard_map/all_to_all | solution.py:328
  94.6 3.6 %all-to-all-start.3 = ((bf16[8,2,6,16,256]{4,3,2,1,0:T(8,128)(2,1)}), bf16[8,2,6,16,256]{4,3,2,1,0:T(8,128)(2,1)S(1)}, u32[]{:S(2)}, u32[]{:S(2)}) async-start(bf16[8,2,6,16,256]{4,3,2,1,0:T(8,128)(2,1)} %fusion.3), calls=%async_computation.3 | async-start | bytes 1572864 | tf_op jit(solution)/shard_map/all_to_all | solution.py:328
  98.3 1.5 copy-done.10
  99.8 14.9 %shard_map.122 = (f32[2,384,256]{2,1,0:T(8,128)S(1)}, bf16[8,2,6,16,256]{4,3,2,1,0:T(8,128)(2,1)}) custom-call(bf16[256,256]{1,0:T(8,128)(2,1)S(1)} %select_convert_fusion.swap_ref, bf16[8,2,6,16,256]{4,3,2,1,0:T(8,128)(2,1)S(1)} %all-to-all-done.x_ref, bf16[2,384,48,256]{3,2,1,0:T(8,128)(2,1)} %bitcast.74, f32[2,384,256]{2,1,0:T(8,128)S(1)} %bitcast.67, ...), custom_call_target="tpu_custom_call" | custom-call | flops 20000000000 | bytes 6291456 | tf_op jit(solution)/shard_map/pallas_call | solution.py:123
  114.6 0.9 copy-done.5
  115.5 3.1 %all-to-all-done.3.x_ref = bf16[8,2,6,16,256]{4,3,2,1,0:T(8,128)(2,1)S(1)} async-done(((bf16[8,2,6,16,256]{4,3,2,1,0:T(8,128)(2,1)}), bf16[8,2,6,16,256]{4,3,2,1,0:T(8,128)(2,1)S(1)}, u32[]{:S(2)}, u32[]{:S(2)}) %all-to-all-start.3) | async-done | bytes 786464 | tf_op jit(solution)/shard_map/all_to_all | solution.py:328
  118.7 1.5 collective-permute-start.4
  120.2 3.7 %all-to-all-start.4 = ((bf16[8,2,6,16,256]{4,3,2,1,0:T(8,128)(2,1)}), bf16[8,2,6,16,256]{4,3,2,1,0:T(8,128)(2,1)S(1)}, u32[]{:S(2)}, u32[]{:S(2)}) async-start(bf16[8,2,6,16,256]{4,3,2,1,0:T(8,128)(2,1)} %collective-permute-done.3), calls=%async_computation.4 | async-start | bytes 1572864 | tf_op jit(solution)/shard_map/all_to_all | solution.py:328
  123.9 1.5 copy-done.11
  125.4 14.0 %shard_map.123 = (f32[2,384,256]{2,1,0:T(8,128)S(1)}, bf16[8,2,6,16,256]{4,3,2,1,0:T(8,128)(2,1)S(1)}) custom-call(bf16[256,256]{1,0:T(8,128)(2,1)S(1)} %select_convert_fusion.swap_ref, bf16[8,2,6,16,256]{4,3,2,1,0:T(8,128)(2,1)S(1)} %all-to-all-done.3.x_ref, bf16[2,384,48,256]{3,2,1,0:T(8,128)(2,1)} %bitcast.75, f32[2,384,256]{2,1,0:T(8,128)S(1)} %bitcast.68, ...), custom_call_target="tpu_custom_call" | custom-call | flops 20000000000 | bytes 6291456 | tf_op jit(solution)/shard_map/pallas_call | solution.py:123
  139.4 0.9 copy-done.6
  140.3 0.9 copy-done.13
  141.2 0.9 copy-done.17
  142.0 1.8 all-to-all-done.4.refs_0_
  143.9 4.0 %all-to-all-start.5 = ((bf16[8,2,6,16,256]{4,3,2,1,0:T(8,128)(2,1)}), bf16[8,2,6,16,256]{4,3,2,1,0:T(8,128)(2,1)S(1)}, u32[]{:S(2)}, u32[]{:S(2)}) async-start(bf16[8,2,6,16,256]{4,3,2,1,0:T(8,128)(2,1)} %copy-done.17), calls=%async_computation.5 | async-start | bytes 1572864 | tf_op jit(solution)/shard_map/all_to_all | solution.py:328
  148.4 18.5 %collective-permute-done.5 = bf16[8,2,6,16,256]{4,3,2,1,0:T(8,128)(2,1)} collective-permute-done((bf16[8,2,6,16,256]{4,3,2,1,0:T(8,128)(2,1)}, bf16[8,2,6,16,256]{4,3,2,1,0:T(8,128)(2,1)}, u32[]{:S(2)}, u32[]{:S(2)}) %collective-permute-start.5) | collective-permute-done | bytes 786464 | tf_op jit(solution)/shard_map/ppermute | solution.py:17
  166.9 0.9 all-to-all-done.5.refs_1_
  167.8 4.8 %all-to-all-start.6 = ((bf16[8,2,6,16,256]{4,3,2,1,0:T(8,128)(2,1)}), bf16[8,2,6,16,256]{4,3,2,1,0:T(8,128)(2,1)S(1)}, u32[]{:S(2)}, u32[]{:S(2)}) async-start(bf16[8,2,6,16,256]{4,3,2,1,0:T(8,128)(2,1)} %collective-permute-done.5), calls=%async_computation.6 | async-start | bytes 1572864 | tf_op jit(solution)/shard_map/all_to_all | solution.py:328
  172.6 1.3 constant_dynamic-slice_fusion.table_ref
  173.9 1.7 add_convert_fusion.1
  176.4 15.3 %all-to-all-done.6.refs_2_ = bf16[8,2,6,16,256]{4,3,2,1,0:T(8,128)(2,1)S(1)} async-done(((bf16[8,2,6,16,256]{4,3,2,1,0:T(8,128)(2,1)}), bf16[8,2,6,16,256]{4,3,2,1,0:T(8,128)(2,1)S(1)}, u32[]{:S(2)}, u32[]{:S(2)}) %all-to-all-start.6) | async-done | bytes 786464 | tf_op jit(solution)/shard_map/all_to_all | solution.py:328
  191.7 4.1 %shard_map.124 = (bf16[6,384,256]{2,1,0:T(8,128)(2,1)S(1)}, bf16[6,384,256]{2,1,0:T(8,128)(2,1)}) custom-call(bf16[768,768]{1,0:T(8,128)(2,1)S(1)} %constant_dynamic-slice_fusion.table_ref, bf16[8,2,6,16,256]{4,3,2,1,0:T(8,128)(2,1)S(1)} %all-to-all-done.4.refs_0_, bf16[8,2,6,16,256]{4,3,2,1,0:T(8,128)(2,1)S(1)} %all-to-all-done.5.refs_1_, ...), custom_call_target="tpu_custom_call" | custom-call | tf_op jit(solution)/shard_map/pallas_call | solution.py:267
  195.8 1.0 copy-done.2
  196.8 3.7 %all-to-all-start.7 = ((bf16[8,96,256]{2,1,0:T(8,128)(2,1)}), bf16[8,96,256]{2,1,0:T(8,128)(2,1)S(1)}, u32[]{:S(2)}, u32[]{:S(2)}) async-start(bf16[8,96,256]{2,1,0:T(8,128)(2,1)} %bitcast.70), calls=%async_computation.7 | async-start | bytes 786432 | tf_op jit(solution)/shard_map/all_to_all | solution.py:328
  200.5 1.1 convert_reduce_fusion
  202.3 10.5 %all-to-all-done.7 = bf16[8,96,256]{2,1,0:T(8,128)(2,1)S(1)} async-done(((bf16[8,96,256]{2,1,0:T(8,128)(2,1)}), bf16[8,96,256]{2,1,0:T(8,128)(2,1)S(1)}, u32[]{:S(2)}, u32[]{:S(2)}) %all-to-all-start.7) | async-done | bytes 393248 | tf_op jit(solution)/shard_map/all_to_all | solution.py:328
  213.7 3.7 %fusion = bf16[1,6,384,512]{3,2,1,0:T(8,128)(2,1)} fusion(bf16[6,384,512]{2,1,0:T(8,128)(2,1)} %collective-permute-done.2, bf16[6,384,256]{2,1,0:T(8,128)(2,1)S(1)} %get-tuple-element.75, bf16[6,384,256]{2,1,0:T(8,128)(2,1)S(1)} %get-tuple-element.74), kind=kLoop, calls=%fused_computation.1 | loop fusion | flops 8257536 | bytes 7077888 | tf_op jit(solution)/shard_map/broadcast_in_dim | solution.py:394
  (45 shorter events, 5.1 us)
Async XLA Ops:
  0.6 1.7 copy-start
  2.3 1.7 copy-start.1
  4.0 1.0 copy-start.7
  5.0 1.0 copy-start.8
  18.4 6.4 %copy-start.15 = (bf16[6,384,256]{2,1,0:T(8,128)(2,1)}, bf16[6,384,256]{2,1,0:T(8,128)(2,1)S(1)}, u32[]{:S(2)}) copy-start(bf16[6,384,256]{2,1,0:T(8,128)(2,1)S(1)} %get-tuple-element.76) | copy-start | bytes 3538948
  18.4 3.3 %collective-permute-start.1 = (bf16[6,384,256]{2,1,0:T(8,128)(2,1)}, bf16[6,384,256]{2,1,0:T(8,128)(2,1)}, u32[]{:S(2)}, u32[]{:S(2)}) collective-permute-start(bf16[6,384,256]{2,1,0:T(8,128)(2,1)} %get-tuple-element.77), channel_id=1, source_target_pairs={{1,0},{0,1},{3,2},{2,3},{5,4},{4,5},{7,6},{6,7},{9,8},{8,9},{11,10... | collective-permute-start | bytes 3538952 | tf_op jit(solution)/shard_map/ppermute | solution.py:17
  24.8 27.6 %all-to-all-start.1 = ((bf16[8,2,6,16,256]{4,3,2,1,0:T(8,128)(2,1)}), bf16[8,2,6,16,256]{4,3,2,1,0:T(8,128)(2,1)S(1)}, u32[]{:S(2)}, u32[]{:S(2)}) async-start(bf16[8,2,6,16,256]{4,3,2,1,0:T(8,128)(2,1)} %fusion.2), calls=%async_computation.1 | async-start | bytes 1572864 | tf_op jit(solution)/shard_map/all_to_all | solution.py:328
  32.1 2.0 collective-permute-start
  32.1 54.0 %collective-permute-start.2 = (bf16[6,384,512]{2,1,0:T(8,128)(2,1)}, bf16[6,384,512]{2,1,0:T(8,128)(2,1)}, u32[]{:S(2)}, u32[]{:S(2)}) collective-permute-start(bf16[6,384,512]{2,1,0:T(8,128)(2,1)} %get-tuple-element.47), channel_id=1, source_target_pairs={{16,0},{0,16},{17,1},{1,17},{18,2},{2,18},{19,3},{3,19},{20,4},{4,... | collective-permute-start | bytes 7077896 | tf_op jit(solution)/shard_map/ppermute | solution.py:17
  34.0 1.3 copy-start.16
  35.3 20.8 %copy-start.12 = (f32[1,2,384,256]{3,2,1,0:T(8,128)S(1)}, f32[1,2,384,256]{3,2,1,0:T(8,128)}, u32[]{:S(2)}) copy-start(f32[1,2,384,256]{3,2,1,0:T(8,128)} %param.12) | copy-start | bytes 2359300
  52.5 24.0 %all-to-all-start = ((bf16[8,2,6,16,256]{4,3,2,1,0:T(8,128)(2,1)}), bf16[8,2,6,16,256]{4,3,2,1,0:T(8,128)(2,1)S(1)}, u32[]{:S(2)}, u32[]{:S(2)}) async-start(bf16[8,2,6,16,256]{4,3,2,1,0:T(8,128)(2,1)} %fusion.1), calls=%async_computation | async-start | bytes 1572864 | tf_op jit(solution)/shard_map/all_to_all | solution.py:328
  56.1 1.5 copy-start.9
  72.4 0.9 copy-start.4
  76.4 18.2 %all-to-all-start.2 = ((bf16[8,128,256]{2,1,0:T(8,128)(2,1)}), bf16[8,128,256]{2,1,0:T(8,128)(2,1)S(1)}, u32[]{:S(2)}, u32[]{:S(2)}) async-start(bf16[8,128,256]{2,1,0:T(8,128)(2,1)} %pad_maximum_fusion), calls=%async_computation.2 | async-start | bytes 1048576 | tf_op jit(solution)/shard_map/all_to_all | solution.py:328
  86.1 32.5 %collective-permute-start.3 = (bf16[8,2,6,16,256]{4,3,2,1,0:T(8,128)(2,1)}, bf16[8,2,6,16,256]{4,3,2,1,0:T(8,128)(2,1)}, u32[]{:S(2)}, u32[]{:S(2)}) collective-permute-start(bf16[8,2,6,16,256]{4,3,2,1,0:T(8,128)(2,1)} %get-tuple-element.49), channel_id=1, source_target_pairs={{16,0},{0,16},{17,1},{1,17},{18,2},{2,18},{19,3},{3,19},{20,4},{4,... | collective-permute-start | bytes 2359304 | tf_op jit(solution)/shard_map/ppermute | solution.py:17
  94.6 20.0 %copy-start.14 = (bf16[8,128,256]{2,1,0:T(8,128)(2,1)}, bf16[8,128,256]{2,1,0:T(8,128)(2,1)S(1)}, u32[]{:S(2)}) copy-start(bf16[8,128,256]{2,1,0:T(8,128)(2,1)S(1)} %all-to-all-done.2) | copy-start | bytes 1572868
  94.6 24.0 %all-to-all-start.3 = ((bf16[8,2,6,16,256]{4,3,2,1,0:T(8,128)(2,1)}), bf16[8,2,6,16,256]{4,3,2,1,0:T(8,128)(2,1)S(1)}, u32[]{:S(2)}, u32[]{:S(2)}) async-start(bf16[8,2,6,16,256]{4,3,2,1,0:T(8,128)(2,1)} %fusion.3), calls=%async_computation.3 | async-start | bytes 1572864 | tf_op jit(solution)/shard_map/all_to_all | solution.py:328
  98.3 1.5 copy-start.10
  114.6 0.9 copy-start.5
  118.7 22.5 %collective-permute-start.4 = (bf16[8,2,6,16,256]{4,3,2,1,0:T(8,128)(2,1)}, bf16[8,2,6,16,256]{4,3,2,1,0:T(8,128)(2,1)S(1)}, u32[]{:S(2)}, u32[]{:S(2)}) collective-permute-start(bf16[8,2,6,16,256]{4,3,2,1,0:T(8,128)(2,1)} %get-tuple-element.56), channel_id=1, source_target_pairs={{16,0},{0,16},{17,1},{1,17},{18,2},{2,18},{19,3},{3,19},{20,4},{4,... | collective-permute-start | bytes 2359304 | tf_op jit(solution)/shard_map/ppermute | solution.py:17
  120.2 23.7 %all-to-all-start.4 = ((bf16[8,2,6,16,256]{4,3,2,1,0:T(8,128)(2,1)}), bf16[8,2,6,16,256]{4,3,2,1,0:T(8,128)(2,1)S(1)}, u32[]{:S(2)}, u32[]{:S(2)}) async-start(bf16[8,2,6,16,256]{4,3,2,1,0:T(8,128)(2,1)} %collective-permute-done.3), calls=%async_computation.4 | async-start | bytes 1572864 | tf_op jit(solution)/shard_map/all_to_all | solution.py:328
  123.9 1.5 copy-start.11
  139.4 0.9 copy-start.6
  140.3 0.9 copy-start.13
  141.2 0.9 copy-start.17
  143.9 23.9 %all-to-all-start.5 = ((bf16[8,2,6,16,256]{4,3,2,1,0:T(8,128)(2,1)}), bf16[8,2,6,16,256]{4,3,2,1,0:T(8,128)(2,1)S(1)}, u32[]{:S(2)}, u32[]{:S(2)}) async-start(bf16[8,2,6,16,256]{4,3,2,1,0:T(8,128)(2,1)} %copy-done.17), calls=%async_computation.5 | async-start | bytes 1572864 | tf_op jit(solution)/shard_map/all_to_all | solution.py:328
  147.8 19.0 %collective-permute-start.5 = (bf16[8,2,6,16,256]{4,3,2,1,0:T(8,128)(2,1)}, bf16[8,2,6,16,256]{4,3,2,1,0:T(8,128)(2,1)}, u32[]{:S(2)}, u32[]{:S(2)}) collective-permute-start(bf16[8,2,6,16,256]{4,3,2,1,0:T(8,128)(2,1)} %copy-done.13), channel_id=1, source_target_pairs={{16,0},{0,16},{17,1},{1,17},{18,2},{2,18},{19,3},{3,19},{20,4},{4,... | collective-permute-start | bytes 2359304 | tf_op jit(solution)/shard_map/ppermute | solution.py:17
  167.8 23.9 %all-to-all-start.6 = ((bf16[8,2,6,16,256]{4,3,2,1,0:T(8,128)(2,1)}), bf16[8,2,6,16,256]{4,3,2,1,0:T(8,128)(2,1)S(1)}, u32[]{:S(2)}, u32[]{:S(2)}) async-start(bf16[8,2,6,16,256]{4,3,2,1,0:T(8,128)(2,1)} %collective-permute-done.5), calls=%async_computation.6 | async-start | bytes 1572864 | tf_op jit(solution)/shard_map/all_to_all | solution.py:328
  195.8 1.0 copy-start.2
  196.8 16.7 %copy-start.3 = (bf16[6,384,256]{2,1,0:T(8,128)(2,1)S(1)}, bf16[6,384,256]{2,1,0:T(8,128)(2,1)}, u32[]{:S(2)}) copy-start(bf16[6,384,256]{2,1,0:T(8,128)(2,1)} %copy-done.2) | copy-start | bytes 3538948
  196.8 16.7 %collective-permute-start.6 = (bf16[6,384,256]{2,1,0:T(8,128)(2,1)}, bf16[6,384,256]{2,1,0:T(8,128)(2,1)S(1)}, u32[]{:S(2)}, u32[]{:S(2)}) collective-permute-start(bf16[6,384,256]{2,1,0:T(8,128)(2,1)} %get-tuple-element.71), channel_id=1, source_target_pairs={{1,0},{0,1},{3,2},{2,3},{5,4},{4,5},{7,6},{6,7},{9,8},{8,9},{11,10... | collective-permute-start | bytes 3538952 | tf_op jit(solution)/shard_map/ppermute | solution.py:17
  196.8 16.0 %all-to-all-start.7 = ((bf16[8,96,256]{2,1,0:T(8,128)(2,1)}), bf16[8,96,256]{2,1,0:T(8,128)(2,1)S(1)}, u32[]{:S(2)}, u32[]{:S(2)}) async-start(bf16[8,96,256]{2,1,0:T(8,128)(2,1)} %bitcast.70), calls=%async_computation.7 | async-start | bytes 786432 | tf_op jit(solution)/shard_map/all_to_all | solution.py:328
